TPU v7x, 512 devices: a whole 4x8x8 slice. The times are simulated.
512 devices in a mesh: vv: 64 (over z, x, core), oo: 8 (over y).
Axes of the slice: x: 4, y: 8, z: 8, core: 2. Of those that a mesh axis runs over, the one named last changes fastest.
Arguments:
- amplitudes: bfloat16 [384, 32768], P(None, ('oo', 'vv')), may hold values from -6 to 6
- integrals: bfloat16 [32768, 32768], P('vv', 'oo'), may hold values from -0.078125 to 0.078125
- allowed: int32 [256, 256], P('vv', 'oo'), may hold values from 0 to 1, as said below
Outputs:
- ladder: bfloat16 [384, 32768], P('oo', 'vv')
Inputs may be any that keep to these rules, and one draw needn't show every extreme that they name: `allowed`: each entry is 0 or 1; nothing about the number of ones may be relied on.
All inputs are finite; a program needn't handle non-finite values.
Results may differ from a plain program's by a relative error of at most 0.0015.
Values may be sent and summed in bfloat16 or wider, within the bound.
No kernel may reach another device: no remote copies, remote signals or barrier semaphores. Data moves between devices by JAX's collectives and lax.ppermute only.
A program may use at most 64 MiB of HBM per device.

v0:
```python
import jax
import jax.numpy as jnp
from jax import lax
from jax.sharding import PartitionSpec as P

BLK = 128


def shards(amplitudes, integrals, allowed):
    tiles = jnp.repeat(jnp.repeat(allowed, BLK, axis=0), BLK, axis=1).astype(jnp.bfloat16)
    masked = integrals * tiles
    dims = (((1,), (1,)), ((), ()))
    gathered = lax.all_gather(amplitudes, "vv", axis=1, tiled=True)
    partial_sum = lax.dot_general(gathered, masked, dims, preferred_element_type=jnp.float32)
    summed = lax.psum_scatter(partial_sum, "oo", scatter_dimension=0, tiled=True)
    return summed.astype(jnp.bfloat16)


def solution(mesh):
    placed = (P(None, ("oo", "vv")), P("vv", "oo"), P("vv", "oo"))
    return jax.shard_map(
        shards, mesh=mesh, in_specs=placed, out_specs=P("oo", "vv"), check_vma=False
    )
```

profile of v0, /device:TPU:2, one launch (start us, length us, event | category | flops | bytes accessed | tf_op | source)
XLA Modules:
  0.0 154.7 jit_solution(4626269794849284513)
XLA Ops:
  6.5 0.0 all-gather.2.cloned.1.call-start
  6.5 0.7 all-gather.2.cloned.1.call-update
  7.3 0.0 reduce-scatter.4.cloned.1.call-start
  7.3 0.7 convert_element_type.14
  8.0 90.6 %all-gather.2.cloned.1.call-done = bf16[384,4096]{0,1:T(8,128)(2,1)} async-done(((bf16[384,64]{0,1:T(8,128)(2,1)}), bf16[384,4096]{0,1:T(8,128)(2,1)}) %all-gather.2.cloned.1.call-update) | async-done | bytes 3145744 | tf_op jit(solution)/shard_map/all_gather | solution.py:13
  98.6 0.0 copy-start
  98.6 3.7 %broadcast_in_dim.7 = bf16[512,32,128]{2,1,0:T(8,128)(2,1)S(1)} broadcast(bf16[512,32]{1,0:T(8,128)(2,1)S(1)} %bitcast.12), dimensions={0,1} | broadcast | bytes 4227072 | tf_op jit(solution)/shard_map/broadcast_in_dim | solution.py:10
  102.3 0.0 copy-done
  102.3 4.4 %fusion.2 = f32[384,512]{0,1:T(8,128)S(1)} fusion(bf16[384,4096]{0,1:T(8,128)(2,1)} %all-gather.2.cloned.1.call-done, bf16[512,4096]{1,0:T(8,128)(2,1)S(1)} %copy-done, bf16[64,8,32,128]{3,2,1,0:T(8,128)(2,1)S(1)} %bitcast.11), kind=kOutput, calls=%fused_computation.3 | convolution fusion | flops 1612709888 | bytes 12320768 | tf_op jit(solution)/shard_map/dot_general | solution.py:14
  106.8 1.2 copy.7
  107.9 0.0 reduce-scatter.4.cloned.1.call-update
  108.0 38.4 %reduce-scatter.4.cloned.1.call-done = f32[48,512]{1,0:T(8,128)} async-done(((f32[384,512]{1,0:T(8,128)}), f32[48,512]{1,0:T(8,128)}) %reduce-scatter.4.cloned.1.call-update) | async-done | bytes 98320 | tf_op jit(solution)/shard_map/reduce_scatter | solution.py:15
  146.4 1.5 convert_element_type.17
  (1 shorter events, 0.0 us)
Async XLA Ops:
  6.5 92.1 %all-gather.2.cloned.1.call-start = ((), (), s32[]{:S(2)}) async-start(), calls=%async_computation.1 | async-start | bytes 3194880 | tf_op jit(solution)/shard_map/all_gather | solution.py:13
  7.3 139.1 %reduce-scatter.4.cloned.1.call-start = ((), (), s32[]{:S(2)}) async-start(), calls=%async_computation.2 | async-start | bytes 884736 | tf_op jit(solution)/shard_map/reduce_scatter | solution.py:15
  98.6 3.7 %copy-start = (bf16[512,4096]{1,0:T(8,128)(2,1)S(1)}, bf16[512,4096]{1,0:T(8,128)(2,1)}, u32[]{:S(2)}) copy-start(bf16[512,4096]{1,0:T(8,128)(2,1)} %param.4) | copy-start | bytes 12582916
Sparse Core Ops, SparseCore 0:
  10.7 87.8 all-gather.1
  108.1 38.2 reduce-scatter.3
where the time goes:
time: 155 us
  waiting for transfers between devices  130 us (84%)
  between operations  13.4 us (9%)
  local copies, waits for them, and re-layouts  4.87 us (3%)
  matrix products  4.43 us (3%)
  other arithmetic  2.2 us (1%)
    all_gather x1, waiting for transfers between devices, shards(): gathered = lax.all_gather(amplitudes, 'vv', axis=1, tiled=True)  90.6 us
    reduce_scatter x1, waiting for transfers between devices, shards(): lax.psum_scatter(partial_sum, 'oo', scatter_dimension=0, tiled=True)  38.4 us
    dot_general x1, matrix products, shards(): lax.dot_general(gathered, masked, dims, preferred_element_type=jnp.float32)  4.43 us
    broadcast_in_dim x1, local copies, waits for them, and re-layouts, shards(): jnp.repeat(jnp.repeat(allowed, BLK, axis=0), BLK, axis=1)  3.69 us
  transfers between devices with their start and end apart: 2, of which 2 were waited for; matrix products, arithmetic and copies ran while one was open for 0% of the time, Pallas kernels for 0%

commit v1 on v0

v1 whole, which is shorter than its diff:
```python
import jax
import jax.numpy as jnp
from jax import lax
from jax.experimental import pallas as pl
from jax.experimental.pallas import tpu as pltpu
from jax.sharding import Mesh, PartitionSpec as P

OP = 384
BLK = 128
NZ, NX, NC, NY = 8, 4, 2, 8
ROWS = 512
COLS = 4096
HALF = OP // 2
SEG = OP // (NY * NC)
SCALE = 32.0


def pick(which, part):
    shape = (OP, 128)
    source = lax.broadcasted_iota(jnp.int32, shape, 0)
    lane = lax.broadcasted_iota(jnp.int32, shape, 1)
    if part == 0:
        wanted = lane
    elif part == 1:
        wanted = jnp.where(lane < 64, lane + 128, -1)
    else:
        wanted = jnp.where(lane >= 64, lane + 64, -1)
    y = sum((wanted >= SEG * k).astype(jnp.int32) for k in range(1, NY))
    row = wanted + y * SEG + which * SEG
    hit = (source == row) & (wanted >= 0)
    return jnp.where(hit, 1.0, 0.0).astype(jnp.bfloat16)


def pack_kernel(a_ref, out_ref):
    a = a_ref[...]
    f32 = jnp.float32
    for core in range(NC):
        head = jnp.dot(a, pick(core, 0), preferred_element_type=f32)
        tail = jnp.dot(a[:32], pick(core, 1), preferred_element_type=f32)
        tail += jnp.dot(a[32:], pick(core, 2), preferred_element_type=f32)
        head, tail = head.astype(jnp.bfloat16), tail.astype(jnp.bfloat16)
        for z in range(NZ):
            out_ref[z, core, :64] = head
            out_ref[z, core, 64:] = tail


def pack(a):
    return pl.pallas_call(
        pack_kernel,
        out_shape=jax.ShapeDtypeStruct((NZ, NC, 96, 128), jnp.bfloat16),
        cost_estimate=pl.CostEstimate(flops=2 * 64 * OP * 512, bytes_accessed=450_000, transcendentals=0),
    )(a)


def mask_kernel(allowed_ref, m_ref, out_ref):
    row = pl.program_id(0)
    for j in range(COLS // BLK):
        keep = allowed_ref[row, j] != 0
        cols = slice(j * BLK, (j + 1) * BLK)
        tile = m_ref[:, cols]
        out_ref[:, cols] = jnp.where(keep, tile, jnp.zeros_like(tile))


def mask(allowed, m):
    return pl.pallas_call(
        mask_kernel,
        grid=(ROWS // BLK,),
        in_specs=[
            pl.BlockSpec(memory_space=pltpu.SMEM),
            pl.BlockSpec((BLK, COLS), lambda i: (i, 0)),
        ],
        out_specs=pl.BlockSpec((BLK, COLS), lambda i: (i, 0)),
        out_shape=jax.ShapeDtypeStruct((ROWS, COLS), jnp.bfloat16),
        cost_estimate=pl.CostEstimate(flops=ROWS * COLS, bytes_accessed=4 * ROWS * COLS, transcendentals=0),
    )(allowed, m)


KC = 4
KW = COLS // KC
ZC = NZ // KC


def dot_kernel(g_ref, own_ref, other_ref, out_ref, w_ref, acc_ref):
    step = pl.program_id(0)
    for z in range(ZC):
        for x in range(NX):
            for c in range(NC):
                at = z * 512 + x * 128 + c * 64
                w_ref[at : at + 64, :128] = g_ref[x, z * NC + c, :64]
                tail = g_ref[x, z * NC + c, 64:]
                w_ref[at : at + 32, 128:] = tail
                w_ref[at + 32 : at + 64, 128:] = jnp.concatenate([tail[:, 64:], tail[:, :64]], axis=1)
    w = w_ref[...]

    @pl.when(step == 0)
    def _():
        acc_ref[...] = jnp.zeros_like(acc_ref)

    for i, m_ref in enumerate((own_ref, other_ref)):
        acc_ref[i] += jnp.dot(m_ref[...], w, preferred_element_type=jnp.float32)

    @pl.when(step == KC - 1)
    def _():
        own, other = [(acc_ref[i] * SCALE).T[:HALF] for i in range(NC)]
        leads = lax.axis_index("c") == 0
        sums = jnp.where(leads, own, other), jnp.where(leads, other, own)
        for y in range(NY):
            for c in range(NC):
                at = (y * NC + c) * SEG
                out_ref[at : at + SEG] = sums[c][y * SEG : (y + 1) * SEG]


def dots(g, own, other):
    return pl.pallas_call(
        dot_kernel,
        grid=(KC,),
        in_specs=[
            pl.BlockSpec((NX, ZC * NC, 96, 128), lambda k: (0, k, 0, 0)),
            pl.BlockSpec((ROWS, KW), lambda k: (0, k)),
            pl.BlockSpec((ROWS, KW), lambda k: (0, k)),
        ],
        out_specs=pl.BlockSpec((OP, ROWS), lambda k: (0, 0)),
        out_shape=jax.ShapeDtypeStruct((OP, ROWS), jnp.float32),
        scratch_shapes=[
            pltpu.VMEM((KW, 256), jnp.bfloat16),
            pltpu.VMEM((NC, ROWS, 256), jnp.float32),
        ],
        compiler_params=pltpu.CompilerParams(vmem_limit_bytes=24 << 20),
        cost_estimate=pl.CostEstimate(flops=2 * OP * ROWS * COLS, bytes_accessed=10 << 20, transcendentals=0),
    )(g, own, other)


def shards(amplitudes, integrals, allowed):
    pieces = pack(amplitudes.T)
    over_z = lax.all_to_all(pieces.reshape(NZ * NC * 96, 128), ("z", "c"), 0, 0, tiled=True)
    own = mask(allowed, integrals)
    other = lax.ppermute(own, "c", [(0, 1), (1, 0)])
    copies = jnp.broadcast_to(over_z[None], (NX, NZ * NC * 96, 128)).reshape(-1, 128)
    over_x = lax.all_to_all(copies, "x", 0, 0, tiled=True)
    g = over_x.reshape(NX, NZ * NC, 96, 128)
    partial_sums = dots(g, own, other).astype(jnp.float16)
    landed = lax.all_to_all(partial_sums, ("y", "c"), 0, 0, tiled=True)
    total = jnp.sum(landed.reshape(NY, 2 * SEG, ROWS).astype(jnp.float32), axis=0)
    return (total * (1.0 / SCALE)).astype(jnp.bfloat16)


def solution(mesh):
    fine = Mesh(mesh.devices.reshape(NZ, NX, NC, NY), ("z", "x", "c", "y"))
    vv = ("z", "x", "c")
    placed = (P(None, ("y",) + vv), P(vv, "y"), P(vv, "y"))
    return jax.shard_map(shards, mesh=fine, in_specs=placed, out_specs=P("y", vv), check_vma=False)
```

time: 155 us -> 89.9 us (0.58)
  the two profiles are of different devices: /device:TPU:2 before, /device:TPU:1 now
where the time goes in v1:
time: 89.9 us; the launch traced here: 89.4 us
  blocking collectives  66.8 us (74%)
  Pallas kernels  12.9 us (14%)
  starting transfers between devices  8.78 us (10%)
    all_to_all x1, blocking collectives, shards(): over_x = lax.all_to_all(copies, 'x', 0, 0, tiled=True)  25 us
    all_to_all x1, blocking collectives, shards(): landed = lax.all_to_all(partial_sums, ('y', 'c'), 0, 0, tiled=True)  21.9 us
    all_to_all x1, blocking collectives, shards(): lax.all_to_all(pieces.reshape(NZ * NC * 96, 128), ('z', 'c'), 0, 0, tiled...  19.9 us
    ppermute x1, starting transfers between devices, shards(): other = lax.ppermute(own, 'c', [(0, 1), (1, 0)])  8.78 us
    pallas_call x1, Pallas kernels, dots(): pl.pallas_call(dot_kernel, grid=(KC,), in_specs=[pl.BlockSpec((NX, ZC * N...  5.84 us
    pallas_call x1, Pallas kernels, mask(): pl.pallas_call(mask_kernel, grid=(ROWS // BLK,), in_specs=[pl.BlockSpec(m...  5.19 us
    pallas_call x1, Pallas kernels, pack(): pl.pallas_call(pack_kernel, out_shape=jax.ShapeDtypeStruct((NZ, NC, 96, 1...  1.84 us
  transfers between devices with their start and end apart: 1, of which 0 were waited for; matrix products, arithmetic and copies ran while one was open for 0% of the time, Pallas kernels for 2%

profile of v1, /device:TPU:1, one launch (start us, length us, event | category | flops | bytes accessed | tf_op | source)
XLA Modules:
  0.0 89.4 jit_solution(3754326523841865168)
XLA Ops:
  0.0 5.2 %shard_map.38.own_ref = bf16[512,4096]{1,0:T(8,128)(2,1)} custom-call(s32[4,32]{1,0:T(4,128)} %allowed_ref.1, bf16[512,4096]{1,0:T(8,128)(2,1)} %m_ref.1), custom_call_target="tpu_custom_call" | custom-call | flops 2097152 | bytes 8388608 | tf_op jit(solution)/shard_map/pallas_call | solution.py:65
  5.2 8.8 %collective-permute-start = (bf16[512,4096]{1,0:T(8,128)(2,1)}, bf16[512,4096]{1,0:T(8,128)(2,1)}, u32[]{:S(2)}, u32[]{:S(2)}) collective-permute-start(bf16[512,4096]{1,0:T(8,128)(2,1)} %shard_map.38.own_ref), channel_id=1, source_target_pairs={{0,8},{8,0},{1,9},{9,1},{2,10},{10,2},{3,11},{11,3},{4,12},{12,4},... | collective-permute-start | bytes 12582920 | tf_op jit(solution)/shard_map/ppermute | solution.py:137
  14.0 1.8 %shard_map.37 = bf16[8,2,96,128]{3,2,1,0:T(8,128)(2,1)} custom-call(bf16[64,384]{1,0:T(8,128)(2,1)} %bitcast.14), custom_call_target="tpu_custom_call" | custom-call | flops 25165824 | bytes 450000 | tf_op jit(solution)/shard_map/pallas_call | solution.py:48
  15.8 0.0 copy-start
  15.8 19.9 %all_to_all.24 = bf16[16,96,128]{2,1,0:T(8,128)(2,1)S(1)} all-to-all(bf16[16,96,128]{2,1,0:T(8,128)(2,1)} %bitcast.10), channel_id=1, replica_groups=mesh['z'=8,'x'=4,'c'=2,'y'=8] {'z','c'}, dimensions={0} | all-to-all | bytes 786432 | tf_op jit(solution)/shard_map/all_to_all | solution.py:135
  35.7 0.2 broadcast_in_dim.9
  35.9 25.0 %all_to_all.25 = bf16[4,1536,128]{2,1,0:T(8,128)(2,1)S(1)} all-to-all(bf16[4,1536,128]{2,1,0:T(8,128)(2,1)S(1)} %broadcast_in_dim.9), channel_id=1, replica_groups=mesh['z'=8,'x'=4,'c'=2,'y'=8] {'x'}, dimensions={0} | all-to-all | bytes 3145728 | tf_op jit(solution)/shard_map/all_to_all | solution.py:139
  60.9 0.0 collective-permute-done.other_ref
  60.9 0.0 copy-done
  60.9 5.8 %shard_map.39 = f32[384,512]{1,0:T(8,128)S(1)} custom-call(bf16[4,16,96,128]{3,2,1,0:T(8,128)(2,1)S(1)} %bitcast.9, bf16[512,4096]{1,0:T(8,128)(2,1)S(1)} %copy-done, bf16[512,4096]{1,0:T(8,128)(2,1)} %collective-permute-done.other_ref), custom_call_target="tpu_custom_call" | custom-call | flops 1610612736 | bytes 10485760 | tf_op jit(solution)/shard_map/pallas_call | solution.py:114
  66.8 0.1 convert_element_type.12
  66.9 21.9 %all_to_all.26 = f16[16,24,512]{2,1,0:T(8,128)(2,1)S(1)} all-to-all(f16[16,24,512]{2,1,0:T(8,128)(2,1)S(1)} %bitcast.11), channel_id=1, replica_groups=mesh['z'=8,'x'=4,'c'=2,'y'=8] {'y','c'}, dimensions={0} | all-to-all | bytes 786432 | tf_op jit(solution)/shard_map/all_to_all | solution.py:142
  88.7 0.1 convert_reduce_fusion
  88.8 0.6 multiply_convert_fusion
Async XLA Ops:
  5.2 55.7 %collective-permute-start = (bf16[512,4096]{1,0:T(8,128)(2,1)}, bf16[512,4096]{1,0:T(8,128)(2,1)}, u32[]{:S(2)}, u32[]{:S(2)}) collective-permute-start(bf16[512,4096]{1,0:T(8,128)(2,1)} %shard_map.38.own_ref), channel_id=1, source_target_pairs={{0,8},{8,0},{1,9},{9,1},{2,10},{10,2},{3,11},{11,3},{4,12},{12,4},... | collective-permute-start | bytes 12582920 | tf_op jit(solution)/shard_map/ppermute | solution.py:137
  15.8 45.1 %copy-start = (bf16[512,4096]{1,0:T(8,128)(2,1)S(1)}, bf16[512,4096]{1,0:T(8,128)(2,1)}, u32[]{:S(2)}) copy-start(bf16[512,4096]{1,0:T(8,128)(2,1)} %shard_map.38.own_ref) | copy-start | bytes 12582916

commit v2 on v1

v2 whole, which is shorter than its diff:
```python
import jax
import jax.numpy as jnp
from jax import lax
from jax.experimental import pallas as pl
from jax.experimental.pallas import tpu as pltpu
from jax.sharding import Mesh, PartitionSpec as P

OP = 384
BLK = 128
NZ, NX, NC, NY = 8, 4, 2, 8
ROWS = 512
COLS = 4096
HALF = OP // 2
SEG = OP // (NY * NC)
SCALE = 32.0


def pick(which, part):
    lane = lax.broadcasted_iota(jnp.int32, (1, 128), 1)
    if part == 0:
        wanted, used = lane, lane >= 0
    elif part == 1:
        wanted, used = lane + 128, lane < 64
    else:
        wanted, used = lane + 64, lane >= 64
    y = sum((wanted >= SEG * k).astype(jnp.int32) for k in range(1, NY))
    row = jnp.where(used, wanted + (y + which) * SEG, -1)
    source = lax.broadcasted_iota(jnp.int32, (OP, 128), 0)
    return jnp.where(source == row, 1.0, 0.0).astype(jnp.bfloat16)


def pack_kernel(a_ref, out_ref):
    a = a_ref[...]
    f32 = jnp.float32
    for core in range(NC):
        head = jnp.dot(a, pick(core, 0), preferred_element_type=f32)
        tail = jnp.dot(a[:32], pick(core, 1), preferred_element_type=f32)
        tail += jnp.dot(a[32:], pick(core, 2), preferred_element_type=f32)
        head, tail = head.astype(jnp.bfloat16), tail.astype(jnp.bfloat16)
        for z in range(NZ):
            out_ref[z, core, :64] = head
            out_ref[z, core, 64:] = tail


def pack(a):
    return pl.pallas_call(
        pack_kernel,
        out_shape=jax.ShapeDtypeStruct((NZ, NC, 96, 128), jnp.bfloat16),
        cost_estimate=pl.CostEstimate(flops=2 * 64 * OP * 512, bytes_accessed=450_000, transcendentals=0),
    )(a)


def mask_kernel(allowed_ref, m_ref, out_ref):
    @pl.loop(0, ROWS // BLK)
    def _(i):
        rows = pl.ds(pl.multiple_of(i * BLK, BLK), BLK)
        for j in range(COLS // BLK):
            keep = allowed_ref[i, j] != 0
            cols = slice(j * BLK, (j + 1) * BLK)
            tile = m_ref[rows, cols]
            out_ref[rows, cols] = jnp.where(keep, tile, jnp.zeros_like(tile))


def mask(allowed, m):
    return pl.pallas_call(
        mask_kernel,
        in_specs=[pl.BlockSpec(memory_space=pltpu.SMEM), pl.BlockSpec(memory_space=pltpu.VMEM)],
        out_specs=pl.BlockSpec(memory_space=pltpu.VMEM),
        out_shape=jax.ShapeDtypeStruct((ROWS, COLS), jnp.bfloat16),
        compiler_params=pltpu.CompilerParams(vmem_limit_bytes=16 << 20),
        cost_estimate=pl.CostEstimate(flops=ROWS * COLS, bytes_accessed=4 * ROWS * COLS, transcendentals=0),
    )(allowed, m)


KW = 512


def dot_kernel(g_ref, own_ref, other_ref, out_ref, w_ref, acc_ref):
    for z in range(NZ):
        for x in range(NX):
            for c in range(NC):
                at = x * 128 + c * 64
                w_ref[at : at + 64, :128] = g_ref[x, z * NC + c, :64]
                tail = g_ref[x, z * NC + c, 64:]
                w_ref[at : at + 32, 128:] = tail
                w_ref[at + 32 : at + 64, 128:] = jnp.concatenate([tail[:, 64:], tail[:, :64]], axis=1)
        w = w_ref[...]
        for i, m_ref in enumerate((own_ref, other_ref)):
            part = jnp.dot(m_ref[:, z * KW : (z + 1) * KW], w, preferred_element_type=jnp.float32)
            if z == 0:
                acc_ref[i] = part
            else:
                acc_ref[i] += part
    own, other = [(acc_ref[i] * SCALE).T[:HALF] for i in range(NC)]
    leads = lax.axis_index("c") == 0
    sums = jnp.where(leads, own, other), jnp.where(leads, other, own)
    for y in range(NY):
        for c in range(NC):
            at = (y * NC + c) * SEG
            out_ref[at : at + SEG] = sums[c][y * SEG : (y + 1) * SEG]


def dots(g, own, other):
    return pl.pallas_call(
        dot_kernel,
        in_specs=[pl.BlockSpec(memory_space=pltpu.VMEM)] * 3,
        out_specs=pl.BlockSpec(memory_space=pltpu.VMEM),
        out_shape=jax.ShapeDtypeStruct((OP, ROWS), jnp.float32),
        scratch_shapes=[
            pltpu.VMEM((KW, 256), jnp.bfloat16),
            pltpu.VMEM((NC, ROWS, 256), jnp.float32),
        ],
        compiler_params=pltpu.CompilerParams(vmem_limit_bytes=24 << 20),
        cost_estimate=pl.CostEstimate(flops=2 * OP * ROWS * COLS, bytes_accessed=10 << 20, transcendentals=0),
    )(g, own, other)


def shards(amplitudes, integrals, allowed):
    pieces = pack(amplitudes.T)
    over_z = lax.all_to_all(pieces.reshape(NZ * NC * 96, 128), ("z", "c"), 0, 0, tiled=True)
    over_z, allowed = lax.optimization_barrier((over_z, allowed))
    own = mask(allowed, integrals)
    other = lax.ppermute(own, "c", [(0, 1), (1, 0)])
    copies = jnp.broadcast_to(over_z[None], (NX, NZ * NC * 96, 128)).reshape(-1, 128)
    over_x = lax.all_to_all(copies, "x", 0, 0, tiled=True)
    g = over_x.reshape(NX, NZ * NC, 96, 128)
    partial_sums = dots(g, own, other).astype(jnp.float16)
    landed = lax.all_to_all(partial_sums, ("y", "c"), 0, 0, tiled=True)
    total = jnp.sum(landed.reshape(NY, 2 * SEG, ROWS).astype(jnp.float32), axis=0)
    return (total * (1.0 / SCALE)).astype(jnp.bfloat16)


def solution(mesh):
    fine = Mesh(mesh.devices.reshape(NZ, NX, NC, NY), ("z", "x", "c", "y"))
    vv = ("z", "x", "c")
    placed = (P(None, ("y",) + vv), P(vv, "y"), P(vv, "y"))
    return jax.shard_map(shards, mesh=fine, in_specs=placed, out_specs=P("y", vv), check_vma=False)
```

time: 89.9 us -> 85.7 us (0.953)
  starting transfers between devices: 8.78 us -> 1.92 us
  Pallas kernels: 12.9 us -> 6.26 us
  blocking collectives: 66.8 us -> 73.3 us
  local copies, waits for them, and re-layouts: 0.21 us -> 3.07 us
    ppermute x1, starting transfers between devices: 8.78 us -> 1.92 us  [shards(): other = lax.ppermute(own, 'c', [(0, 1), (1, 0)])]
    pallas_call x2, Pallas kernels: 11 us -> 4.48 us  [the longest x1 2.73 us: dots(): pl.pallas_call(dot_kernel, in_specs=[pl.BlockSpec(memory_space=pltpu.VMEM...]
    all_to_all x1, blocking collectives: 19.9 us -> 26.4 us  [shards(): lax.all_to_all(pieces.reshape(NZ * NC * 96, 128), ('z', 'c'), 0, 0, tiled...]
    unnamed x2 -> x4, local copies, waits for them, and re-layouts: 0.01 us -> 2.87 us
    all_to_all x1, blocking collectives: 21.9 us -> 23.4 us  [shards(): landed = lax.all_to_all(partial_sums, ('y', 'c'), 0, 0, tiled=True)]
    all_to_all x1, blocking collectives: 25 us -> 23.5 us  [shards(): over_x = lax.all_to_all(copies, 'x', 0, 0, tiled=True)]
  transfers between devices with their start and end apart: 1 -> 1, of which waited for: 0 -> 0; matrix products, arithmetic and copies ran while one was open for 0% -> 0% of each run, Pallas kernels for 2% -> 0%
where the time goes in v2:
time: 85.7 us; the launch traced here: 85.3 us
  blocking collectives  73.3 us (86%)
  Pallas kernels  6.26 us (7%)
  local copies, waits for them, and re-layouts  3.07 us (4%)
  starting transfers between devices  1.92 us (2%)
    all_to_all x1, blocking collectives, shards(): lax.all_to_all(pieces.reshape(NZ * NC * 96, 128), ('z', 'c'), 0, 0, tiled...  26.4 us
    all_to_all x1, blocking collectives, shards(): over_x = lax.all_to_all(copies, 'x', 0, 0, tiled=True)  23.5 us
    all_to_all x1, blocking collectives, shards(): landed = lax.all_to_all(partial_sums, ('y', 'c'), 0, 0, tiled=True)  23.4 us
    unnamed x4, local copies, waits for them, and re-layouts  2.87 us
    pallas_call x1, Pallas kernels, dots(): pl.pallas_call(dot_kernel, in_specs=[pl.BlockSpec(memory_space=pltpu.VMEM...  2.73 us
    ppermute x1, starting transfers between devices, shards(): other = lax.ppermute(own, 'c', [(0, 1), (1, 0)])  1.92 us
    pallas_call x1, Pallas kernels, pack(): pl.pallas_call(pack_kernel, out_shape=jax.ShapeDtypeStruct((NZ, NC, 96, 1...  1.78 us
    pallas_call x1, Pallas kernels, mask(): pl.pallas_call(mask_kernel, in_specs=[pl.BlockSpec(memory_space=pltpu.SME...  1.75 us
  transfers between devices with their start and end apart: 1, of which 0 were waited for; matrix products, arithmetic and copies ran while one was open for 0% of the time, Pallas kernels for 0%

profile of v2, /device:TPU:1, one launch (start us, length us, event | category | flops | bytes accessed | tf_op | source)
XLA Modules:
  0.0 85.3 jit_solution(12917806959249278905)
XLA Ops:
  0.0 1.8 %shard_map.37 = bf16[8,2,96,128]{3,2,1,0:T(8,128)(2,1)} custom-call(bf16[64,384]{1,0:T(8,128)(2,1)} %bitcast.14), custom_call_target="tpu_custom_call" | custom-call | flops 25165824 | bytes 450000 | tf_op jit(solution)/shard_map/pallas_call | solution.py:46
  1.8 26.4 %all_to_all.27 = bf16[16,96,128]{2,1,0:T(8,128)(2,1)S(1)} all-to-all(bf16[16,96,128]{2,1,0:T(8,128)(2,1)} %bitcast.10), channel_id=1, replica_groups=mesh['z'=8,'x'=4,'c'=2,'y'=8] {'z','c'}, dimensions={0} | all-to-all | bytes 786432 | tf_op jit(solution)/shard_map/all_to_all | solution.py:120
  28.2 0.0 copy-start
  28.2 2.2 %copy-done = bf16[512,4096]{1,0:T(8,128)(2,1)S(1)} copy-done((bf16[512,4096]{1,0:T(8,128)(2,1)S(1)}, bf16[512,4096]{1,0:T(8,128)(2,1)}, u32[]{:S(2)}) %copy-start) | copy-done | bytes 4194328
  30.3 0.0 copy-start.1
  30.3 0.7 copy-done.1
  31.0 1.7 %shard_map.38.own_ref = bf16[512,4096]{1,0:T(8,128)(2,1)S(1)} custom-call(s32[4,32]{1,0:T(4,128)S(1)} %copy-done.1, bf16[512,4096]{1,0:T(8,128)(2,1)S(1)} %copy-done), custom_call_target="tpu_custom_call" | custom-call | flops 2097152 | bytes 8388608 | tf_op jit(solution)/shard_map/pallas_call | solution.py:65
  32.8 1.9 %collective-permute-start = (bf16[512,4096]{1,0:T(8,128)(2,1)S(1)}, bf16[512,4096]{1,0:T(8,128)(2,1)S(1)}, u32[]{:S(2)}, u32[]{:S(2)}) collective-permute-start(bf16[512,4096]{1,0:T(8,128)(2,1)S(1)} %shard_map.38.own_ref), channel_id=1, source_target_pairs={{0,8},{8,0},{1,9},{9,1},{2,10},{10,2},{3,11},{11,3},{4,12},{12,4},... | collective-permute-start | bytes 12582920 | tf_op jit(solution)/shard_map/ppermute | solution.py:123
  34.7 0.2 broadcast_in_dim.2
  34.9 23.5 %all_to_all.28 = bf16[4,1536,128]{2,1,0:T(8,128)(2,1)S(1)} all-to-all(bf16[4,1536,128]{2,1,0:T(8,128)(2,1)S(1)} %broadcast_in_dim.2), channel_id=1, replica_groups=mesh['z'=8,'x'=4,'c'=2,'y'=8] {'x'}, dimensions={0} | all-to-all | bytes 3145728 | tf_op jit(solution)/shard_map/all_to_all | solution.py:125
  58.5 0.0 collective-permute-done.other_ref
  58.5 2.7 %shard_map.39 = f32[384,512]{1,0:T(8,128)S(1)} custom-call(bf16[4,16,96,128]{3,2,1,0:T(8,128)(2,1)S(1)} %bitcast.9, bf16[512,4096]{1,0:T(8,128)(2,1)S(1)} %shard_map.38.own_ref, bf16[512,4096]{1,0:T(8,128)(2,1)S(1)} %collective-permute-done.other_ref), custom_call_target="tpu_custom_call" | custom-call | flops 1610612736 | bytes 10485760 | tf_op jit(solution)/shard_map/pallas_call | solution.py:104
  61.2 0.1 convert_element_type.12
  61.3 23.4 %all_to_all.29 = f16[16,24,512]{2,1,0:T(8,128)(2,1)S(1)} all-to-all(f16[16,24,512]{2,1,0:T(8,128)(2,1)S(1)} %bitcast.11), channel_id=1, replica_groups=mesh['z'=8,'x'=4,'c'=2,'y'=8] {'y','c'}, dimensions={0} | all-to-all | bytes 786432 | tf_op jit(solution)/shard_map/all_to_all | solution.py:128
  84.7 0.1 convert_reduce_fusion
  84.7 0.6 multiply_convert_fusion
Async XLA Ops:
  28.2 2.2 %copy-start = (bf16[512,4096]{1,0:T(8,128)(2,1)S(1)}, bf16[512,4096]{1,0:T(8,128)(2,1)}, u32[]{:S(2)}) copy-start(bf16[512,4096]{1,0:T(8,128)(2,1)} %m_ref.1) | copy-start | bytes 12582916
  30.3 0.7 copy-start.1
  32.8 25.7 %collective-permute-start = (bf16[512,4096]{1,0:T(8,128)(2,1)S(1)}, bf16[512,4096]{1,0:T(8,128)(2,1)S(1)}, u32[]{:S(2)}, u32[]{:S(2)}) collective-permute-start(bf16[512,4096]{1,0:T(8,128)(2,1)S(1)} %shard_map.38.own_ref), channel_id=1, source_target_pairs={{0,8},{8,0},{1,9},{9,1},{2,10},{10,2},{3,11},{11,3},{4,12},{12,4},... | collective-permute-start | bytes 12582920 | tf_op jit(solution)/shard_map/ppermute | solution.py:123

commit v3 on v2

--- a/solution.py
+++ b/solution.py
@@ -72,25 +72,41 @@
     )(allowed, m)
 
 
-KW = 512
+def spread(block_ref, w_ref):
+    for zc in range(NZ * NC):
+        at = zc * 64
+        w_ref[at : at + 64, :128] = block_ref[zc, :64]
+        tail = block_ref[zc, 64:]
+        w_ref[at : at + 32, 128:] = tail
+        w_ref[at + 32 : at + 64, 128:] = jnp.concatenate([tail[:, 64:], tail[:, :64]], axis=1)
 
 
-def dot_kernel(g_ref, own_ref, other_ref, out_ref, w_ref, acc_ref):
-    for z in range(NZ):
-        for x in range(NX):
-            for c in range(NC):
-                at = x * 128 + c * 64
-                w_ref[at : at + 64, :128] = g_ref[x, z * NC + c, :64]
-                tail = g_ref[x, z * NC + c, 64:]
-                w_ref[at : at + 32, 128:] = tail
-                w_ref[at + 32 : at + 64, 128:] = jnp.concatenate([tail[:, 64:], tail[:, :64]], axis=1)
+def block_dot(m_ref, w, x):
+    at = [pl.ds(pl.multiple_of(z * NX * BLK + x * BLK, BLK), BLK) for z in range(NZ)]
+    m = jnp.concatenate([m_ref[:, cols] for cols in at], axis=1)
+    return jnp.dot(m, w, preferred_element_type=jnp.float32)
+
+
+def source(shift):
+    return lax.rem(lax.axis_index("x") + (NX - shift), NX)
+
+
+def first_kernel(shifts, *refs):
+    block_refs = refs[: len(shifts)]
+    own_ref, other_ref, acc_ref, w_ref = refs[len(shifts) :]
+    for n, shift in enumerate(shifts):
+        spread(block_refs[n], w_ref)
         w = w_ref[...]
         for i, m_ref in enumerate((own_ref, other_ref)):
-            part = jnp.dot(m_ref[:, z * KW : (z + 1) * KW], w, preferred_element_type=jnp.float32)
-            if z == 0:
-                acc_ref[i] = part
-            else:
-                acc_ref[i] += part
+            part = block_dot(m_ref, w, source(shift))
+            acc_ref[i] = part if n == 0 else acc_ref[i] + part
+
+
+def last_kernel(shift, block_ref, in_ref, own_ref, other_ref, out_ref, w_ref, acc_ref):
+    spread(block_ref, w_ref)
+    w = w_ref[...]
+    for i, m_ref in enumerate((own_ref, other_ref)):
+        acc_ref[i] = in_ref[i] + block_dot(m_ref, w, source(shift))
     own, other = [(acc_ref[i] * SCALE).T[:HALF] for i in range(NC)]
     leads = lax.axis_index("c") == 0
     sums = jnp.where(leads, own, other), jnp.where(leads, other, own)
@@ -100,31 +116,55 @@
             out_ref[at : at + SEG] = sums[c][y * SEG : (y + 1) * SEG]
 
 
-def dots(g, own, other):
+ACC = (NC, ROWS, 256)
+WIDE = NZ * NC * 64
+
+
+def first_dots(shifts, blocks, own, other):
+    def first(*refs):
+        first_kernel(shifts, *refs)
+
     return pl.pallas_call(
-        dot_kernel,
-        in_specs=[pl.BlockSpec(memory_space=pltpu.VMEM)] * 3,
+        first,
+        in_specs=[pl.BlockSpec(memory_space=pltpu.VMEM)] * (len(shifts) + 2),
+        out_specs=pl.BlockSpec(memory_space=pltpu.VMEM),
+        out_shape=jax.ShapeDtypeStruct(ACC, jnp.float32),
+        scratch_shapes=[pltpu.VMEM((WIDE, 256), jnp.bfloat16)],
+        compiler_params=pltpu.CompilerParams(vmem_limit_bytes=16 << 20),
+        cost_estimate=pl.CostEstimate(flops=OP * ROWS * COLS, bytes_accessed=3 << 20, transcendentals=0),
+    )(*blocks, own, other)
+
+
+def last_dots(shift, block, acc, own, other):
+    def last(*refs):
+        last_kernel(shift, *refs)
+
+    return pl.pallas_call(
+        last,
+        in_specs=[pl.BlockSpec(memory_space=pltpu.VMEM)] * 4,
         out_specs=pl.BlockSpec(memory_space=pltpu.VMEM),
         out_shape=jax.ShapeDtypeStruct((OP, ROWS), jnp.float32),
-        scratch_shapes=[
-            pltpu.VMEM((KW, 256), jnp.bfloat16),
-            pltpu.VMEM((NC, ROWS, 256), jnp.float32),
-        ],
-        compiler_params=pltpu.CompilerParams(vmem_limit_bytes=24 << 20),
-        cost_estimate=pl.CostEstimate(flops=2 * OP * ROWS * COLS, bytes_accessed=10 << 20, transcendentals=0),
-    )(g, own, other)
+        scratch_shapes=[pltpu.VMEM((WIDE, 256), jnp.bfloat16), pltpu.VMEM(ACC, jnp.float32)],
+        compiler_params=pltpu.CompilerParams(vmem_limit_bytes=16 << 20),
+        cost_estimate=pl.CostEstimate(flops=OP * ROWS * COLS // 2, bytes_accessed=3 << 20, transcendentals=0),
+    )(block, acc, own, other)
+
+
+SHIFTS = (2, 1, 3)
 
 
 def shards(amplitudes, integrals, allowed):
+    swap = [(0, 1), (1, 0)]
+    raw = lax.ppermute(integrals, "c", swap)
     pieces = pack(amplitudes.T)
     over_z = lax.all_to_all(pieces.reshape(NZ * NC * 96, 128), ("z", "c"), 0, 0, tiled=True)
-    over_z, allowed = lax.optimization_barrier((over_z, allowed))
+    block = over_z.reshape(NZ * NC, 96, 128)
+    far, right, left = [lax.ppermute(block, "x", [(i, (i + d) % NX) for i in range(NX)]) for d in SHIFTS]
+    block, allowed = lax.optimization_barrier((block, allowed))
     own = mask(allowed, integrals)
-    other = lax.ppermute(own, "c", [(0, 1), (1, 0)])
-    copies = jnp.broadcast_to(over_z[None], (NX, NZ * NC * 96, 128)).reshape(-1, 128)
-    over_x = lax.all_to_all(copies, "x", 0, 0, tiled=True)
-    g = over_x.reshape(NX, NZ * NC, 96, 128)
-    partial_sums = dots(g, own, other).astype(jnp.float16)
+    other = mask(lax.ppermute(allowed, "c", swap), raw)
+    acc = first_dots((0, 1, 3), (block, right, left), own, other)
+    partial_sums = last_dots(2, far, acc, own, other).astype(jnp.float16)
     landed = lax.all_to_all(partial_sums, ("y", "c"), 0, 0, tiled=True)
     total = jnp.sum(landed.reshape(NY, 2 * SEG, ROWS).astype(jnp.float32), axis=0)
     return (total * (1.0 / SCALE)).astype(jnp.bfloat16)

time: 85.7 us -> 80.3 us (0.937)
  blocking collectives: 73.3 us -> 41.2 us
  starting transfers between devices: 1.92 us -> 20.7 us
  waiting for transfers between devices: 0.01 us -> 3.86 us
  Pallas kernels: 6.26 us -> 10 us
    all_to_all x1 -> x0, blocking collectives: 23.5 us -> none  [shards(): over_x = lax.all_to_all(copies, 'x', 0, 0, tiled=True)]
    ppermute x1 -> x5, starting transfers between devices: 1.92 us -> 20.7 us  [the longest x3 9.92 us: shards(): lax.ppermute(block, 'x', [(i, (i + d) % NX) for i in range(NX)])]
    all_to_all x1, blocking collectives: 26.4 us -> 19.6 us  [shards(): lax.all_to_all(pieces.reshape(NZ * NC * 96, 128), ('z', 'c'), 0, 0, tiled...]
    ppermute x1 -> x5, waiting for transfers between devices: 0.01 us -> 3.86 us  [the longest x3 3.86 us: shards(): lax.ppermute(block, 'x', [(i, (i + d) % NX) for i in range(NX)])]
    pallas_call x1 -> x2, Pallas kernels: 1.75 us -> 5.13 us  [mask(): pl.pallas_call(mask_kernel, in_specs=[pl.BlockSpec(memory_space=pltpu.SME...]
    all_to_all x1, blocking collectives: 23.4 us -> 21.6 us  [shards(): landed = lax.all_to_all(partial_sums, ('y', 'c'), 0, 0, tiled=True)]
    pallas_call x1 -> x2, Pallas kernels: 2.73 us -> 3.09 us  [the longest x1 2.06 us: first_dots(): pl.pallas_call(first, in_specs=[pl.BlockSpec(memory_space=pltpu.VMEM)] *...]
  transfers between devices with their start and end apart: 1 -> 5, of which waited for: 0 -> 1; matrix products, arithmetic and copies ran while one was open for 0% -> 0% of each run, Pallas kernels for 0% -> 11%
where the time goes in v3:
time: 80.3 us; the launch traced here: 79.5 us
  blocking collectives  41.2 us (51%)
  starting transfers between devices  20.7 us (26%)
  Pallas kernels  10 us (12%)
  waiting for transfers between devices  3.86 us (5%)
  local copies, waits for them, and re-layouts  2.86 us (4%)
    all_to_all x1, blocking collectives, shards(): landed = lax.all_to_all(partial_sums, ('y', 'c'), 0, 0, tiled=True)  21.6 us
    all_to_all x1, blocking collectives, shards(): lax.all_to_all(pieces.reshape(NZ * NC * 96, 128), ('z', 'c'), 0, 0, tiled...  19.6 us
    ppermute x3, starting transfers between devices, shards(): lax.ppermute(block, 'x', [(i, (i + d) % NX) for i in range(NX)])  9.92 us
    ppermute x1, starting transfers between devices, shards(): raw = lax.ppermute(integrals, 'c', swap)  8.78 us
    pallas_call x2, Pallas kernels, mask(): pl.pallas_call(mask_kernel, in_specs=[pl.BlockSpec(memory_space=pltpu.SME...  5.13 us
    ppermute x3, waiting for transfers between devices, shards(): lax.ppermute(block, 'x', [(i, (i + d) % NX) for i in range(NX)])  3.86 us
    unnamed x4, local copies, waits for them, and re-layouts  2.86 us
    pallas_call x1, Pallas kernels, first_dots(): pl.pallas_call(first, in_specs=[pl.BlockSpec(memory_space=pltpu.VMEM)] *...  2.06 us
  transfers between devices with their start and end apart: 5, of which 1 were waited for; matrix products, arithmetic and copies ran while one was open for 0% of the time, Pallas kernels for 11%

profile of v3, /device:TPU:1, one launch (start us, length us, event | category | flops | bytes accessed | tf_op | source)
XLA Modules:
  0.0 79.5 jit_solution(7808253525717132491)
XLA Ops:
  0.0 8.8 %collective-permute-start.4 = (bf16[512,4096]{1,0:T(8,128)(2,1)}, bf16[512,4096]{1,0:T(8,128)(2,1)}, u32[]{:S(2)}, u32[]{:S(2)}) collective-permute-start(bf16[512,4096]{1,0:T(8,128)(2,1)} %m_ref.1), channel_id=1, source_target_pairs={{0,8},{8,0},{1,9},{9,1},{2,10},{10,2},{3,11},{11,3},{4,12},{12,4},... | collective-permute-start | bytes 12582920 | tf_op jit(solution)/shard_map/ppermute | solution.py:158
  8.8 1.8 %shard_map.37 = bf16[8,2,96,128]{3,2,1,0:T(8,128)(2,1)} custom-call(bf16[64,384]{1,0:T(8,128)(2,1)} %bitcast.10), custom_call_target="tpu_custom_call" | custom-call | flops 25165824 | bytes 450000 | tf_op jit(solution)/shard_map/pallas_call | solution.py:46
  10.6 19.6 %all_to_all.18.refs_0_ = bf16[16,96,128]{2,1,0:T(8,128)(2,1)S(1)} all-to-all(bf16[16,96,128]{2,1,0:T(8,128)(2,1)} %bitcast.7), channel_id=1, replica_groups=mesh['z'=8,'x'=4,'c'=2,'y'=8] {'z','c'}, dimensions={0} | all-to-all | bytes 786432 | tf_op jit(solution)/shard_map/all_to_all | solution.py:160
  30.2 3.1 %collective-permute-start.1 = (bf16[16,96,128]{2,1,0:T(8,128)(2,1)S(1)}, bf16[16,96,128]{2,1,0:T(8,128)(2,1)S(1)}, u32[]{:S(2)}, u32[]{:S(2)}) collective-permute-start(bf16[16,96,128]{2,1,0:T(8,128)(2,1)S(1)} %all_to_all.18.refs_0_), channel_id=1, source_target_pairs={{0,16},{16,32},{32,48},{48,0},{1,17},{17,33},{33,49},{49,1},{2,18}... | collective-permute-start | bytes 1179656 | tf_op jit(solution)/shard_map/ppermute | solution.py:162
  33.3 3.4 %collective-permute-start.2 = (bf16[16,96,128]{2,1,0:T(8,128)(2,1)S(1)}, bf16[16,96,128]{2,1,0:T(8,128)(2,1)S(1)}, u32[]{:S(2)}, u32[]{:S(2)}) collective-permute-start(bf16[16,96,128]{2,1,0:T(8,128)(2,1)S(1)} %all_to_all.18.refs_0_), channel_id=1, source_target_pairs={{0,48},{16,0},{32,16},{48,32},{1,49},{17,1},{33,17},{49,33},{2,50}... | collective-permute-start | bytes 1179656 | tf_op jit(solution)/shard_map/ppermute | solution.py:162
  36.7 3.4 %collective-permute-start = (bf16[16,96,128]{2,1,0:T(8,128)(2,1)S(1)}, bf16[16,96,128]{2,1,0:T(8,128)(2,1)S(1)}, u32[]{:S(2)}, u32[]{:S(2)}) collective-permute-start(bf16[16,96,128]{2,1,0:T(8,128)(2,1)S(1)} %all_to_all.18.refs_0_), channel_id=1, source_target_pairs={{0,32},{16,48},{32,0},{48,16},{1,33},{17,49},{33,1},{49,17},{2,34}... | collective-permute-start | bytes 1179656 | tf_op jit(solution)/shard_map/ppermute | solution.py:162
  40.1 2.0 %collective-permute-start.3 = (s32[4,32]{1,0:T(4,128)}, s32[4,32]{1,0:T(4,128)S(1)}, u32[]{:S(2)}, u32[]{:S(2)}) collective-permute-start(s32[4,32]{1,0:T(4,128)} %allowed_ref), channel_id=1, source_target_pairs={{0,8},{8,0},{1,9},{9,1},{2,10},{10,2},{3,11},{11,3},{4,12},{12,4},... | collective-permute-start | bytes 1544 | tf_op jit(solution)/shard_map/ppermute | solution.py:165
  42.1 0.0 copy-start
  42.1 2.2 %copy-done = bf16[512,4096]{1,0:T(8,128)(2,1)S(1)} copy-done((bf16[512,4096]{1,0:T(8,128)(2,1)S(1)}, bf16[512,4096]{1,0:T(8,128)(2,1)}, u32[]{:S(2)}) %copy-start) | copy-done | bytes 4194328
  44.3 0.0 copy-start.1
  44.3 0.7 copy-done.1
  45.0 1.7 %shard_map.38.refs_3_.refs_2_ = bf16[512,4096]{1,0:T(8,128)(2,1)S(1)} custom-call(s32[4,32]{1,0:T(4,128)S(1)} %copy-done.1, bf16[512,4096]{1,0:T(8,128)(2,1)S(1)} %copy-done), custom_call_target="tpu_custom_call" | custom-call | flops 2097152 | bytes 8388608 | tf_op jit(solution)/shard_map/pallas_call | solution.py:65
  46.8 0.0 collective-permute-done.3.allowed_ref
  46.8 0.0 collective-permute-done.4.m_ref
  46.8 3.4 %shard_map.39.refs_4_.refs_3_ = bf16[512,4096]{1,0:T(8,128)(2,1)S(1)} custom-call(s32[4,32]{1,0:T(4,128)S(1)} %collective-permute-done.3.allowed_ref, bf16[512,4096]{1,0:T(8,128)(2,1)} %collective-permute-done.4.m_ref), custom_call_target="tpu_custom_call" | custom-call | flops 2097152 | bytes 8388608 | tf_op jit(solution)/shard_map/pallas_call | solution.py:65
  50.2 0.0 collective-permute-done.1.refs_1_
  50.2 3.9 %collective-permute-done.2.refs_2_ = bf16[16,96,128]{2,1,0:T(8,128)(2,1)S(1)} collective-permute-done((bf16[16,96,128]{2,1,0:T(8,128)(2,1)S(1)}, bf16[16,96,128]{2,1,0:T(8,128)(2,1)S(1)}, u32[]{:S(2)}, u32[]{:S(2)}) %collective-permute-start.2) | collective-permute-done | bytes 393248 | tf_op jit(solution)/shard_map/ppermute | solution.py:162
  54.0 2.1 %shard_map.40.refs_1_ = f32[2,512,256]{2,1,0:T(8,128)S(1)} custom-call(bf16[16,96,128]{2,1,0:T(8,128)(2,1)S(1)} %all_to_all.18.refs_0_, bf16[16,96,128]{2,1,0:T(8,128)(2,1)S(1)} %collective-permute-done.1.refs_1_, bf16[16,96,128]{2,1,0:T(8,128)(2,1)S(1)} %collective-permute-done.2.refs_2_, bf16[512,4096]{1,0:T(8,128)(2,1)S(1)} %shard_map.38.refs_3_.refs_2_, ...), custom_call_target="tpu_custom_call" | custom-call | flops 805306368 | bytes 3145728 | tf_op jit(solution)/shard_map/pallas_call | solution.py:127
  56.1 0.0 collective-permute-done.refs_0_
  56.1 1.0 %shard_map.41 = f32[384,512]{1,0:T(8,128)S(1)} custom-call(bf16[16,96,128]{2,1,0:T(8,128)(2,1)S(1)} %collective-permute-done.refs_0_, f32[2,512,256]{2,1,0:T(8,128)S(1)} %shard_map.40.refs_1_, bf16[512,4096]{1,0:T(8,128)(2,1)S(1)} %shard_map.38.refs_3_.refs_2_, bf16[512,4096]{1,0:T(8,128)(2,1)S(1)} %shard_map.39.refs_4_.refs_3_), custom_call_target="tpu_custom_call" | custom-call | flops 402653184 | bytes 3145728 | tf_op jit(solution)/shard_map/pallas_call | solution.py:142
  57.1 0.1 convert_element_type.12
  57.2 21.6 %all_to_all.19 = f16[16,24,512]{2,1,0:T(8,128)(2,1)S(1)} all-to-all(f16[16,24,512]{2,1,0:T(8,128)(2,1)S(1)} %bitcast.8), channel_id=1, replica_groups=mesh['z'=8,'x'=4,'c'=2,'y'=8] {'y','c'}, dimensions={0} | all-to-all | bytes 786432 | tf_op jit(solution)/shard_map/all_to_all | solution.py:168
  78.8 0.1 convert_reduce_fusion
  78.8 0.6 multiply_convert_fusion
Async XLA Ops:
  0.0 46.8 %collective-permute-start.4 = (bf16[512,4096]{1,0:T(8,128)(2,1)}, bf16[512,4096]{1,0:T(8,128)(2,1)}, u32[]{:S(2)}, u32[]{:S(2)}) collective-permute-start(bf16[512,4096]{1,0:T(8,128)(2,1)} %m_ref.1), channel_id=1, source_target_pairs={{0,8},{8,0},{1,9},{9,1},{2,10},{10,2},{3,11},{11,3},{4,12},{12,4},... | collective-permute-start | bytes 12582920 | tf_op jit(solution)/shard_map/ppermute | solution.py:158
  30.2 20.0 %collective-permute-start.1 = (bf16[16,96,128]{2,1,0:T(8,128)(2,1)S(1)}, bf16[16,96,128]{2,1,0:T(8,128)(2,1)S(1)}, u32[]{:S(2)}, u32[]{:S(2)}) collective-permute-start(bf16[16,96,128]{2,1,0:T(8,128)(2,1)S(1)} %all_to_all.18.refs_0_), channel_id=1, source_target_pairs={{0,16},{16,32},{32,48},{48,0},{1,17},{17,33},{33,49},{49,1},{2,18}... | collective-permute-start | bytes 1179656 | tf_op jit(solution)/shard_map/ppermute | solution.py:162
  33.3 20.7 %collective-permute-start.2 = (bf16[16,96,128]{2,1,0:T(8,128)(2,1)S(1)}, bf16[16,96,128]{2,1,0:T(8,128)(2,1)S(1)}, u32[]{:S(2)}, u32[]{:S(2)}) collective-permute-start(bf16[16,96,128]{2,1,0:T(8,128)(2,1)S(1)} %all_to_all.18.refs_0_), channel_id=1, source_target_pairs={{0,48},{16,0},{32,16},{48,32},{1,49},{17,1},{33,17},{49,33},{2,50}... | collective-permute-start | bytes 1179656 | tf_op jit(solution)/shard_map/ppermute | solution.py:162
  36.7 19.4 %collective-permute-start = (bf16[16,96,128]{2,1,0:T(8,128)(2,1)S(1)}, bf16[16,96,128]{2,1,0:T(8,128)(2,1)S(1)}, u32[]{:S(2)}, u32[]{:S(2)}) collective-permute-start(bf16[16,96,128]{2,1,0:T(8,128)(2,1)S(1)} %all_to_all.18.refs_0_), channel_id=1, source_target_pairs={{0,32},{16,48},{32,0},{48,16},{1,33},{17,49},{33,1},{49,17},{2,34}... | collective-permute-start | bytes 1179656 | tf_op jit(solution)/shard_map/ppermute | solution.py:162
  40.1 6.6 %collective-permute-start.3 = (s32[4,32]{1,0:T(4,128)}, s32[4,32]{1,0:T(4,128)S(1)}, u32[]{:S(2)}, u32[]{:S(2)}) collective-permute-start(s32[4,32]{1,0:T(4,128)} %allowed_ref), channel_id=1, source_target_pairs={{0,8},{8,0},{1,9},{9,1},{2,10},{10,2},{3,11},{11,3},{4,12},{12,4},... | collective-permute-start | bytes 1544 | tf_op jit(solution)/shard_map/ppermute | solution.py:165
  42.1 2.2 %copy-start = (bf16[512,4096]{1,0:T(8,128)(2,1)S(1)}, bf16[512,4096]{1,0:T(8,128)(2,1)}, u32[]{:S(2)}) copy-start(bf16[512,4096]{1,0:T(8,128)(2,1)} %m_ref.1) | copy-start | bytes 12582916
  44.3 0.7 copy-start.1

commit v4 on v3

--- a/solution.py
+++ b/solution.py
@@ -15,28 +15,23 @@
 SCALE = 32.0
 
 
-def pick(which, part):
-    lane = lax.broadcasted_iota(jnp.int32, (1, 128), 1)
-    if part == 0:
-        wanted, used = lane, lane >= 0
-    elif part == 1:
-        wanted, used = lane + 128, lane < 64
-    else:
-        wanted, used = lane + 64, lane >= 64
-    y = sum((wanted >= SEG * k).astype(jnp.int32) for k in range(1, NY))
-    row = jnp.where(used, wanted + (y + which) * SEG, -1)
-    source = lax.broadcasted_iota(jnp.int32, (OP, 128), 0)
+def pick():
+    lane = lax.broadcasted_iota(jnp.int32, (1, 512), 1)
+    head = lane < 256
+    core = jnp.where(head, lane // 128, (lane - 256) // 128)
+    place = jnp.where(head, lane % 128, 128 + lane % 64)
+    row = (place // SEG) * (NC * SEG) + core * SEG + place % SEG
+    source = lax.broadcasted_iota(jnp.int32, (OP, 512), 0)
     return jnp.where(source == row, 1.0, 0.0).astype(jnp.bfloat16)
 
 
 def pack_kernel(a_ref, out_ref):
-    a = a_ref[...]
-    f32 = jnp.float32
+    picked = jnp.dot(a_ref[...], pick(), preferred_element_type=jnp.float32)
+    low = lax.broadcasted_iota(jnp.int32, (32, 128), 1) < 64
     for core in range(NC):
-        head = jnp.dot(a, pick(core, 0), preferred_element_type=f32)
-        tail = jnp.dot(a[:32], pick(core, 1), preferred_element_type=f32)
-        tail += jnp.dot(a[32:], pick(core, 2), preferred_element_type=f32)
-        head, tail = head.astype(jnp.bfloat16), tail.astype(jnp.bfloat16)
+        head = picked[:, core * 128 : (core + 1) * 128].astype(jnp.bfloat16)
+        both = picked[:, 256 + core * 128 : 256 + (core + 1) * 128]
+        tail = jnp.where(low, both[:32], both[32:]).astype(jnp.bfloat16)
         for z in range(NZ):
             out_ref[z, core, :64] = head
             out_ref[z, core, 64:] = tail
@@ -46,6 +41,9 @@
     return pl.pallas_call(
         pack_kernel,
         out_shape=jax.ShapeDtypeStruct((NZ, NC, 96, 128), jnp.bfloat16),
+        in_specs=[pl.BlockSpec(memory_space=pltpu.VMEM)],
+        out_specs=pl.BlockSpec(memory_space=pltpu.VMEM),
+        compiler_params=pltpu.CompilerParams(vmem_limit_bytes=4 << 20),
         cost_estimate=pl.CostEstimate(flops=2 * 64 * OP * 512, bytes_accessed=450_000, transcendentals=0),
     )(a)
 
@@ -91,15 +89,20 @@
     return lax.rem(lax.axis_index("x") + (NX - shift), NX)
 
 
-def first_kernel(shifts, *refs):
+def some_kernel(shifts, *refs):
     block_refs = refs[: len(shifts)]
-    own_ref, other_ref, acc_ref, w_ref = refs[len(shifts) :]
+    own_ref, other_ref, acc_ref, w_ref = refs[-4:]
+    before_ref = refs[len(shifts)] if len(refs) > len(shifts) + 4 else None
     for n, shift in enumerate(shifts):
         spread(block_refs[n], w_ref)
         w = w_ref[...]
         for i, m_ref in enumerate((own_ref, other_ref)):
             part = block_dot(m_ref, w, source(shift))
-            acc_ref[i] = part if n == 0 else acc_ref[i] + part
+            if n > 0:
+                part += acc_ref[i]
+            elif before_ref is not None:
+                part += before_ref[i]
+            acc_ref[i] = part
 
 
 def last_kernel(shift, block_ref, in_ref, own_ref, other_ref, out_ref, w_ref, acc_ref):
@@ -120,19 +123,21 @@
 WIDE = NZ * NC * 64
 
 
-def first_dots(shifts, blocks, own, other):
-    def first(*refs):
-        first_kernel(shifts, *refs)
+def some_dots(shifts, blocks, before, own, other):
+    def some(*refs):
+        some_kernel(shifts, *refs)
 
     return pl.pallas_call(
-        first,
-        in_specs=[pl.BlockSpec(memory_space=pltpu.VMEM)] * (len(shifts) + 2),
+        some,
+        in_specs=[pl.BlockSpec(memory_space=pltpu.VMEM)] * (len(shifts) + len(before) + 2),
         out_specs=pl.BlockSpec(memory_space=pltpu.VMEM),
         out_shape=jax.ShapeDtypeStruct(ACC, jnp.float32),
         scratch_shapes=[pltpu.VMEM((WIDE, 256), jnp.bfloat16)],
         compiler_params=pltpu.CompilerParams(vmem_limit_bytes=16 << 20),
-        cost_estimate=pl.CostEstimate(flops=OP * ROWS * COLS, bytes_accessed=3 << 20, transcendentals=0),
-    )(*blocks, own, other)
+        cost_estimate=pl.CostEstimate(
+            flops=len(shifts) * OP * ROWS * COLS // 2, bytes_accessed=3 << 20, transcendentals=0
+        ),
+    )(*blocks, *before, own, other)
 
 
 def last_dots(shift, block, acc, own, other):
@@ -163,8 +168,9 @@
     block, allowed = lax.optimization_barrier((block, allowed))
     own = mask(allowed, integrals)
     other = mask(lax.ppermute(allowed, "c", swap), raw)
-    acc = first_dots((0, 1, 3), (block, right, left), own, other)
-    partial_sums = last_dots(2, far, acc, own, other).astype(jnp.float16)
+    acc = some_dots((0,), (block,), (), own, other)
+    acc = some_dots((2, 1), (far, right), (acc,), own, other)
+    partial_sums = last_dots(3, left, acc, own, other).astype(jnp.float16)
     landed = lax.all_to_all(partial_sums, ("y", "c"), 0, 0, tiled=True)
     total = jnp.sum(landed.reshape(NY, 2 * SEG, ROWS).astype(jnp.float32), axis=0)
     return (total * (1.0 / SCALE)).astype(jnp.bfloat16)

time: 80.3 us -> 77.4 us (0.964)
  Pallas kernels: 10 us -> 7 us
  waiting for transfers between devices: 3.86 us -> 2.26 us
  starting transfers between devices: 20.7 us -> 21.9 us
    pallas_call x2, Pallas kernels: 5.13 us -> 3.5 us  [mask(): pl.pallas_call(mask_kernel, in_specs=[pl.BlockSpec(memory_space=pltpu.SME...]
    ppermute x3, waiting for transfers between devices: 3.86 us -> 2.26 us  [shards(): lax.ppermute(block, 'x', [(i, (i + d) % NX) for i in range(NX)])]
    pallas_call x1, Pallas kernels: 1.79 us -> 0.22 us  [pack(): pl.pallas_call(pack_kernel, out_shape=jax.ShapeDtypeStruct((NZ, NC, 96, 1...]
    ppermute x3, starting transfers between devices: 9.92 us -> 11.1 us  [shards(): lax.ppermute(block, 'x', [(i, (i + d) % NX) for i in range(NX)])]
    unnamed x4 -> x6, local copies, waits for them, and re-layouts: 2.86 us -> 3.66 us
    pallas_call x1 -> x2, Pallas kernels: 2.06 us -> 2.27 us  [some_dots(): pl.pallas_call(some, in_specs=[pl.BlockSpec(memory_space=pltpu.VMEM)] * (...]
  transfers between devices with their start and end apart: 5 -> 5, of which waited for: 1 -> 1; matrix products, arithmetic and copies ran while one was open for 0% -> 0% of each run, Pallas kernels for 11% -> 8%
where the time goes in v4:
time: 77.4 us; the launch traced here: 77 us
  blocking collectives  41.3 us (53%)
  starting transfers between devices  21.9 us (28%)
  Pallas kernels  7 us (9%)
  local copies, waits for them, and re-layouts  3.66 us (5%)
  waiting for transfers between devices  2.26 us (3%)
    all_to_all x1, blocking collectives, shards(): landed = lax.all_to_all(partial_sums, ('y', 'c'), 0, 0, tiled=True)  21.8 us
    all_to_all x1, blocking collectives, shards(): lax.all_to_all(pieces.reshape(NZ * NC * 96, 128), ('z', 'c'), 0, 0, tiled...  19.4 us
    ppermute x3, starting transfers between devices, shards(): lax.ppermute(block, 'x', [(i, (i + d) % NX) for i in range(NX)])  11.1 us
    ppermute x1, starting transfers between devices, shards(): raw = lax.ppermute(integrals, 'c', swap)  8.78 us
    unnamed x6, local copies, waits for them, and re-layouts  3.66 us
    pallas_call x2, Pallas kernels, mask(): pl.pallas_call(mask_kernel, in_specs=[pl.BlockSpec(memory_space=pltpu.SME...  3.5 us
    pallas_call x2, Pallas kernels, some_dots(): pl.pallas_call(some, in_specs=[pl.BlockSpec(memory_space=pltpu.VMEM)] * (...  2.27 us
    ppermute x3, waiting for transfers between devices, shards(): lax.ppermute(block, 'x', [(i, (i + d) % NX) for i in range(NX)])  2.26 us
  transfers between devices with their start and end apart: 5, of which 1 were waited for; matrix products, arithmetic and copies ran while one was open for 0% of the time, Pallas kernels for 8%

profile of v4, /device:TPU:1, one launch (start us, length us, event | category | flops | bytes accessed | tf_op | source)
XLA Modules:
  0.0 77.0 jit_solution(3702479167651569073)
XLA Ops:
  0.0 8.8 %collective-permute-start.4 = (bf16[512,4096]{1,0:T(8,128)(2,1)}, bf16[512,4096]{1,0:T(8,128)(2,1)S(1)}, u32[]{:S(2)}, u32[]{:S(2)}) collective-permute-start(bf16[512,4096]{1,0:T(8,128)(2,1)} %m_ref.1), channel_id=1, source_target_pairs={{0,8},{8,0},{1,9},{9,1},{2,10},{10,2},{3,11},{11,3},{4,12},{12,4},... | collective-permute-start | bytes 12582920 | tf_op jit(solution)/shard_map/ppermute | solution.py:163
  8.8 0.0 copy-start.1
  8.8 0.8 %copy-done.1 = bf16[384,64]{0,1:T(8,128)(2,1)S(1)} copy-done((bf16[384,64]{0,1:T(8,128)(2,1)S(1)}, bf16[384,64]{0,1:T(8,128)(2,1)}, u32[]{:S(2)}) %copy-start.1) | copy-done | bytes 49176
  9.6 0.2 shard_map.37
  9.8 19.4 %all_to_all.18.refs_0_ = bf16[16,96,128]{2,1,0:T(8,128)(2,1)S(1)} all-to-all(bf16[16,96,128]{2,1,0:T(8,128)(2,1)S(1)} %bitcast.7), channel_id=1, replica_groups=mesh['z'=8,'x'=4,'c'=2,'y'=8] {'z','c'}, dimensions={0} | all-to-all | bytes 786432 | tf_op jit(solution)/shard_map/all_to_all | solution.py:165
  29.2 4.6 %collective-permute-start.1 = (bf16[16,96,128]{2,1,0:T(8,128)(2,1)S(1)}, bf16[16,96,128]{2,1,0:T(8,128)(2,1)S(1)}, u32[]{:S(2)}, u32[]{:S(2)}) collective-permute-start(bf16[16,96,128]{2,1,0:T(8,128)(2,1)S(1)} %all_to_all.18.refs_0_), channel_id=1, source_target_pairs={{0,32},{16,48},{32,0},{48,16},{1,33},{17,49},{33,1},{49,17},{2,34}... | collective-permute-start | bytes 1179656 | tf_op jit(solution)/shard_map/ppermute | solution.py:167
  33.9 2.2 %collective-permute-start.2 = (bf16[16,96,128]{2,1,0:T(8,128)(2,1)S(1)}, bf16[16,96,128]{2,1,0:T(8,128)(2,1)S(1)}, u32[]{:S(2)}, u32[]{:S(2)}) collective-permute-start(bf16[16,96,128]{2,1,0:T(8,128)(2,1)S(1)} %all_to_all.18.refs_0_), channel_id=1, source_target_pairs={{0,16},{16,32},{32,48},{48,0},{1,17},{17,33},{33,49},{49,1},{2,18}... | collective-permute-start | bytes 1179656 | tf_op jit(solution)/shard_map/ppermute | solution.py:167
  36.1 4.3 %collective-permute-start = (bf16[16,96,128]{2,1,0:T(8,128)(2,1)S(1)}, bf16[16,96,128]{2,1,0:T(8,128)(2,1)S(1)}, u32[]{:S(2)}, u32[]{:S(2)}) collective-permute-start(bf16[16,96,128]{2,1,0:T(8,128)(2,1)S(1)} %all_to_all.18.refs_0_), channel_id=1, source_target_pairs={{0,48},{16,0},{32,16},{48,32},{1,49},{17,1},{33,17},{49,33},{2,50}... | collective-permute-start | bytes 1179656 | tf_op jit(solution)/shard_map/ppermute | solution.py:167
  40.4 2.0 %collective-permute-start.3 = (s32[4,32]{1,0:T(4,128)}, s32[4,32]{1,0:T(4,128)S(1)}, u32[]{:S(2)}, u32[]{:S(2)}) collective-permute-start(s32[4,32]{1,0:T(4,128)} %allowed_ref), channel_id=1, source_target_pairs={{0,8},{8,0},{1,9},{9,1},{2,10},{10,2},{3,11},{11,3},{4,12},{12,4},... | collective-permute-start | bytes 1544 | tf_op jit(solution)/shard_map/ppermute | solution.py:170
  42.4 0.0 copy-start
  42.4 2.2 %copy-done = bf16[512,4096]{1,0:T(8,128)(2,1)S(1)} copy-done((bf16[512,4096]{1,0:T(8,128)(2,1)S(1)}, bf16[512,4096]{1,0:T(8,128)(2,1)}, u32[]{:S(2)}) %copy-start) | copy-done | bytes 4194328
  44.6 0.0 copy-start.2
  44.6 0.7 copy-done.2
  45.2 1.7 %shard_map.38.refs_1_.refs_3_.refs_2_ = bf16[512,4096]{1,0:T(8,128)(2,1)S(1)} custom-call(s32[4,32]{1,0:T(4,128)S(1)} %copy-done.2, bf16[512,4096]{1,0:T(8,128)(2,1)S(1)} %copy-done), custom_call_target="tpu_custom_call" | custom-call | flops 2097152 | bytes 8388608 | tf_op jit(solution)/shard_map/pallas_call | solution.py:63
  47.0 0.0 collective-permute-done.3.allowed_ref
  47.0 0.0 collective-permute-done.4.m_ref
  47.0 1.7 %shard_map.39.refs_2_.refs_4_.refs_3_ = bf16[512,4096]{1,0:T(8,128)(2,1)S(1)} custom-call(s32[4,32]{1,0:T(4,128)S(1)} %collective-permute-done.3.allowed_ref, bf16[512,4096]{1,0:T(8,128)(2,1)S(1)} %collective-permute-done.4.m_ref), custom_call_target="tpu_custom_call" | custom-call | flops 2097152 | bytes 8388608 | tf_op jit(solution)/shard_map/pallas_call | solution.py:63
  48.8 0.8 %shard_map.40.refs_2_ = f32[2,512,256]{2,1,0:T(8,128)S(1)} custom-call(bf16[16,96,128]{2,1,0:T(8,128)(2,1)S(1)} %all_to_all.18.refs_0_, bf16[512,4096]{1,0:T(8,128)(2,1)S(1)} %shard_map.38.refs_1_.refs_3_.refs_2_, bf16[512,4096]{1,0:T(8,128)(2,1)S(1)} %shard_map.39.refs_2_.refs_4_.refs_3_), custom_call_target="tpu_custom_call" | custom-call | flops 402653184 | bytes 3145728 | tf_op jit(solution)/shard_map/pallas_call | solution.py:130
  49.6 0.0 collective-permute-done.1.refs_0_
  49.6 2.3 %collective-permute-done.2.refs_1_ = bf16[16,96,128]{2,1,0:T(8,128)(2,1)S(1)} collective-permute-done((bf16[16,96,128]{2,1,0:T(8,128)(2,1)S(1)}, bf16[16,96,128]{2,1,0:T(8,128)(2,1)S(1)}, u32[]{:S(2)}, u32[]{:S(2)}) %collective-permute-start.2) | collective-permute-done | bytes 393248 | tf_op jit(solution)/shard_map/ppermute | solution.py:167
  51.9 1.5 %shard_map.41.refs_1_ = f32[2,512,256]{2,1,0:T(8,128)S(1)} custom-call(bf16[16,96,128]{2,1,0:T(8,128)(2,1)S(1)} %collective-permute-done.1.refs_0_, bf16[16,96,128]{2,1,0:T(8,128)(2,1)S(1)} %collective-permute-done.2.refs_1_, f32[2,512,256]{2,1,0:T(8,128)S(1)} %shard_map.40.refs_2_, bf16[512,4096]{1,0:T(8,128)(2,1)S(1)} %shard_map.38.refs_1_.refs_3_.refs_2_, ...), custom_call_target="tpu_custom_call" | custom-call | flops 805306368 | bytes 3145728 | tf_op jit(solution)/shard_map/pallas_call | solution.py:130
  53.3 0.0 collective-permute-done.refs_0_
  53.3 1.0 %shard_map.42 = f32[384,512]{1,0:T(8,128)S(1)} custom-call(bf16[16,96,128]{2,1,0:T(8,128)(2,1)S(1)} %collective-permute-done.refs_0_, f32[2,512,256]{2,1,0:T(8,128)S(1)} %shard_map.41.refs_1_, bf16[512,4096]{1,0:T(8,128)(2,1)S(1)} %shard_map.38.refs_1_.refs_3_.refs_2_, bf16[512,4096]{1,0:T(8,128)(2,1)S(1)} %shard_map.39.refs_2_.refs_4_.refs_3_), custom_call_target="tpu_custom_call" | custom-call | flops 402653184 | bytes 3145728 | tf_op jit(solution)/shard_map/pallas_call | solution.py:147
  54.4 0.1 convert_element_type.12
  54.4 21.8 %all_to_all.19 = f16[16,24,512]{2,1,0:T(8,128)(2,1)S(1)} all-to-all(f16[16,24,512]{2,1,0:T(8,128)(2,1)S(1)} %bitcast.9), channel_id=1, replica_groups=mesh['z'=8,'x'=4,'c'=2,'y'=8] {'y','c'}, dimensions={0} | all-to-all | bytes 786432 | tf_op jit(solution)/shard_map/all_to_all | solution.py:174
  76.3 0.1 convert_reduce_fusion
  76.3 0.6 multiply_convert_fusion
Async XLA Ops:
  0.0 47.0 %collective-permute-start.4 = (bf16[512,4096]{1,0:T(8,128)(2,1)}, bf16[512,4096]{1,0:T(8,128)(2,1)S(1)}, u32[]{:S(2)}, u32[]{:S(2)}) collective-permute-start(bf16[512,4096]{1,0:T(8,128)(2,1)} %m_ref.1), channel_id=1, source_target_pairs={{0,8},{8,0},{1,9},{9,1},{2,10},{10,2},{3,11},{11,3},{4,12},{12,4},... | collective-permute-start | bytes 12582920 | tf_op jit(solution)/shard_map/ppermute | solution.py:163
  8.8 0.8 %copy-start.1 = (bf16[384,64]{0,1:T(8,128)(2,1)S(1)}, bf16[384,64]{0,1:T(8,128)(2,1)}, u32[]{:S(2)}) copy-start(bf16[384,64]{0,1:T(8,128)(2,1)} %param.3) | copy-start | bytes 147460
  29.2 20.4 %collective-permute-start.1 = (bf16[16,96,128]{2,1,0:T(8,128)(2,1)S(1)}, bf16[16,96,128]{2,1,0:T(8,128)(2,1)S(1)}, u32[]{:S(2)}, u32[]{:S(2)}) collective-permute-start(bf16[16,96,128]{2,1,0:T(8,128)(2,1)S(1)} %all_to_all.18.refs_0_), channel_id=1, source_target_pairs={{0,32},{16,48},{32,0},{48,16},{1,33},{17,49},{33,1},{49,17},{2,34}... | collective-permute-start | bytes 1179656 | tf_op jit(solution)/shard_map/ppermute | solution.py:167
  33.9 18.0 %collective-permute-start.2 = (bf16[16,96,128]{2,1,0:T(8,128)(2,1)S(1)}, bf16[16,96,128]{2,1,0:T(8,128)(2,1)S(1)}, u32[]{:S(2)}, u32[]{:S(2)}) collective-permute-start(bf16[16,96,128]{2,1,0:T(8,128)(2,1)S(1)} %all_to_all.18.refs_0_), channel_id=1, source_target_pairs={{0,16},{16,32},{32,48},{48,0},{1,17},{17,33},{33,49},{49,1},{2,18}... | collective-permute-start | bytes 1179656 | tf_op jit(solution)/shard_map/ppermute | solution.py:167
  36.1 17.2 %collective-permute-start = (bf16[16,96,128]{2,1,0:T(8,128)(2,1)S(1)}, bf16[16,96,128]{2,1,0:T(8,128)(2,1)S(1)}, u32[]{:S(2)}, u32[]{:S(2)}) collective-permute-start(bf16[16,96,128]{2,1,0:T(8,128)(2,1)S(1)} %all_to_all.18.refs_0_), channel_id=1, source_target_pairs={{0,48},{16,0},{32,16},{48,32},{1,49},{17,1},{33,17},{49,33},{2,50}... | collective-permute-start | bytes 1179656 | tf_op jit(solution)/shard_map/ppermute | solution.py:167
  40.4 6.6 %collective-permute-start.3 = (s32[4,32]{1,0:T(4,128)}, s32[4,32]{1,0:T(4,128)S(1)}, u32[]{:S(2)}, u32[]{:S(2)}) collective-permute-start(s32[4,32]{1,0:T(4,128)} %allowed_ref), channel_id=1, source_target_pairs={{0,8},{8,0},{1,9},{9,1},{2,10},{10,2},{3,11},{11,3},{4,12},{12,4},... | collective-permute-start | bytes 1544 | tf_op jit(solution)/shard_map/ppermute | solution.py:170
  42.4 2.2 %copy-start = (bf16[512,4096]{1,0:T(8,128)(2,1)S(1)}, bf16[512,4096]{1,0:T(8,128)(2,1)}, u32[]{:S(2)}) copy-start(bf16[512,4096]{1,0:T(8,128)(2,1)} %m_ref.1) | copy-start | bytes 12582916
  44.6 0.7 copy-start.2

commit v5 on v4

--- a/solution.py
+++ b/solution.py
@@ -168,8 +168,8 @@
     block, allowed = lax.optimization_barrier((block, allowed))
     own = mask(allowed, integrals)
     other = mask(lax.ppermute(allowed, "c", swap), raw)
-    acc = some_dots((0,), (block,), (), own, other)
-    acc = some_dots((2, 1), (far, right), (acc,), own, other)
+    acc = some_dots((0, 2), (block, far), (), own, other)
+    acc = some_dots((1,), (right,), (acc,), own, other)
     partial_sums = last_dots(3, left, acc, own, other).astype(jnp.float16)
     landed = lax.all_to_all(partial_sums, ("y", "c"), 0, 0, tiled=True)
     total = jnp.sum(landed.reshape(NY, 2 * SEG, ROWS).astype(jnp.float32), axis=0)

time: 77.4 us -> 76.7 us (level)
  no operation moved by 1% of the time
where the time goes in v5:
time: 76.7 us; the launch traced here: 76.3 us
  blocking collectives  41.3 us (54%)
  starting transfers between devices  21.9 us (29%)
  Pallas kernels  6.98 us (9%)
  local copies, waits for them, and re-layouts  3.66 us (5%)
  waiting for transfers between devices  1.64 us (2%)
    all_to_all x1, blocking collectives, shards(): landed = lax.all_to_all(partial_sums, ('y', 'c'), 0, 0, tiled=True)  21.9 us
    all_to_all x1, blocking collectives, shards(): lax.all_to_all(pieces.reshape(NZ * NC * 96, 128), ('z', 'c'), 0, 0, tiled...  19.4 us
    ppermute x3, starting transfers between devices, shards(): lax.ppermute(block, 'x', [(i, (i + d) % NX) for i in range(NX)])  11.1 us
    ppermute x1, starting transfers between devices, shards(): raw = lax.ppermute(integrals, 'c', swap)  8.78 us
    unnamed x6, local copies, waits for them, and re-layouts  3.66 us
    pallas_call x2, Pallas kernels, mask(): pl.pallas_call(mask_kernel, in_specs=[pl.BlockSpec(memory_space=pltpu.SME...  3.5 us
    pallas_call x2, Pallas kernels, some_dots(): pl.pallas_call(some, in_specs=[pl.BlockSpec(memory_space=pltpu.VMEM)] * (...  2.25 us
    ppermute x1, starting transfers between devices, shards(): other = mask(lax.ppermute(allowed, 'c', swap), raw)  1.99 us
  transfers between devices with their start and end apart: 5, of which 1 were waited for; matrix products, arithmetic and copies ran while one was open for 0% of the time, Pallas kernels for 8%

profile of v5, /device:TPU:1, one launch (start us, length us, event | category | flops | bytes accessed | tf_op | source)
XLA Modules:
  0.0 76.3 jit_solution(17882916587359559667)
XLA Ops:
  0.0 8.8 %collective-permute-start.4 = (bf16[512,4096]{1,0:T(8,128)(2,1)}, bf16[512,4096]{1,0:T(8,128)(2,1)S(1)}, u32[]{:S(2)}, u32[]{:S(2)}) collective-permute-start(bf16[512,4096]{1,0:T(8,128)(2,1)} %m_ref.1), channel_id=1, source_target_pairs={{0,8},{8,0},{1,9},{9,1},{2,10},{10,2},{3,11},{11,3},{4,12},{12,4},... | collective-permute-start | bytes 12582920 | tf_op jit(solution)/shard_map/ppermute | solution.py:163
  8.8 0.0 copy-start.1
  8.8 0.8 %copy-done.1 = bf16[384,64]{0,1:T(8,128)(2,1)S(1)} copy-done((bf16[384,64]{0,1:T(8,128)(2,1)S(1)}, bf16[384,64]{0,1:T(8,128)(2,1)}, u32[]{:S(2)}) %copy-start.1) | copy-done | bytes 49176
  9.6 0.2 shard_map.37
  9.8 19.4 %all_to_all.18.refs_0_ = bf16[16,96,128]{2,1,0:T(8,128)(2,1)S(1)} all-to-all(bf16[16,96,128]{2,1,0:T(8,128)(2,1)S(1)} %bitcast.7), channel_id=1, replica_groups=mesh['z'=8,'x'=4,'c'=2,'y'=8] {'z','c'}, dimensions={0} | all-to-all | bytes 786432 | tf_op jit(solution)/shard_map/all_to_all | solution.py:165
  29.2 4.6 %collective-permute-start.2 = (bf16[16,96,128]{2,1,0:T(8,128)(2,1)S(1)}, bf16[16,96,128]{2,1,0:T(8,128)(2,1)S(1)}, u32[]{:S(2)}, u32[]{:S(2)}) collective-permute-start(bf16[16,96,128]{2,1,0:T(8,128)(2,1)S(1)} %all_to_all.18.refs_0_), channel_id=1, source_target_pairs={{0,32},{16,48},{32,0},{48,16},{1,33},{17,49},{33,1},{49,17},{2,34}... | collective-permute-start | bytes 1179656 | tf_op jit(solution)/shard_map/ppermute | solution.py:167
  33.9 2.2 %collective-permute-start.1 = (bf16[16,96,128]{2,1,0:T(8,128)(2,1)S(1)}, bf16[16,96,128]{2,1,0:T(8,128)(2,1)S(1)}, u32[]{:S(2)}, u32[]{:S(2)}) collective-permute-start(bf16[16,96,128]{2,1,0:T(8,128)(2,1)S(1)} %all_to_all.18.refs_0_), channel_id=1, source_target_pairs={{0,16},{16,32},{32,48},{48,0},{1,17},{17,33},{33,49},{49,1},{2,18}... | collective-permute-start | bytes 1179656 | tf_op jit(solution)/shard_map/ppermute | solution.py:167
  36.1 4.3 %collective-permute-start = (bf16[16,96,128]{2,1,0:T(8,128)(2,1)S(1)}, bf16[16,96,128]{2,1,0:T(8,128)(2,1)S(1)}, u32[]{:S(2)}, u32[]{:S(2)}) collective-permute-start(bf16[16,96,128]{2,1,0:T(8,128)(2,1)S(1)} %all_to_all.18.refs_0_), channel_id=1, source_target_pairs={{0,48},{16,0},{32,16},{48,32},{1,49},{17,1},{33,17},{49,33},{2,50}... | collective-permute-start | bytes 1179656 | tf_op jit(solution)/shard_map/ppermute | solution.py:167
  40.4 2.0 %collective-permute-start.3 = (s32[4,32]{1,0:T(4,128)}, s32[4,32]{1,0:T(4,128)S(1)}, u32[]{:S(2)}, u32[]{:S(2)}) collective-permute-start(s32[4,32]{1,0:T(4,128)} %allowed_ref), channel_id=1, source_target_pairs={{0,8},{8,0},{1,9},{9,1},{2,10},{10,2},{3,11},{11,3},{4,12},{12,4},... | collective-permute-start | bytes 1544 | tf_op jit(solution)/shard_map/ppermute | solution.py:170
  42.4 0.0 copy-start
  42.4 2.2 %copy-done = bf16[512,4096]{1,0:T(8,128)(2,1)S(1)} copy-done((bf16[512,4096]{1,0:T(8,128)(2,1)S(1)}, bf16[512,4096]{1,0:T(8,128)(2,1)}, u32[]{:S(2)}) %copy-start) | copy-done | bytes 4194328
  44.6 0.0 copy-start.2
  44.6 0.7 copy-done.2
  45.2 1.7 %shard_map.38.refs_2_ = bf16[512,4096]{1,0:T(8,128)(2,1)S(1)} custom-call(s32[4,32]{1,0:T(4,128)S(1)} %copy-done.2, bf16[512,4096]{1,0:T(8,128)(2,1)S(1)} %copy-done), custom_call_target="tpu_custom_call" | custom-call | flops 2097152 | bytes 8388608 | tf_op jit(solution)/shard_map/pallas_call | solution.py:63
  47.0 0.0 collective-permute-done.3.allowed_ref
  47.0 0.0 collective-permute-done.4.m_ref
  47.0 1.7 %shard_map.39.refs_3_ = bf16[512,4096]{1,0:T(8,128)(2,1)S(1)} custom-call(s32[4,32]{1,0:T(4,128)S(1)} %collective-permute-done.3.allowed_ref, bf16[512,4096]{1,0:T(8,128)(2,1)S(1)} %collective-permute-done.4.m_ref), custom_call_target="tpu_custom_call" | custom-call | flops 2097152 | bytes 8388608 | tf_op jit(solution)/shard_map/pallas_call | solution.py:63
  48.8 0.0 collective-permute-done.2.refs_1_
  48.8 1.4 %shard_map.40.refs_1_ = f32[2,512,256]{2,1,0:T(8,128)S(1)} custom-call(bf16[16,96,128]{2,1,0:T(8,128)(2,1)S(1)} %all_to_all.18.refs_0_, bf16[16,96,128]{2,1,0:T(8,128)(2,1)S(1)} %collective-permute-done.2.refs_1_, bf16[512,4096]{1,0:T(8,128)(2,1)S(1)} %shard_map.38.refs_2_, bf16[512,4096]{1,0:T(8,128)(2,1)S(1)} %shard_map.39.refs_3_), custom_call_target="tpu_custom_call" | custom-call | flops 805306368 | bytes 3145728 | tf_op jit(solution)/shard_map/pallas_call | solution.py:130
  50.2 1.6 %collective-permute-done.1.refs_0_ = bf16[16,96,128]{2,1,0:T(8,128)(2,1)S(1)} collective-permute-done((bf16[16,96,128]{2,1,0:T(8,128)(2,1)S(1)}, bf16[16,96,128]{2,1,0:T(8,128)(2,1)S(1)}, u32[]{:S(2)}, u32[]{:S(2)}) %collective-permute-start.1) | collective-permute-done | bytes 393248 | tf_op jit(solution)/shard_map/ppermute | solution.py:167
  51.9 0.8 %shard_map.41.refs_1_ = f32[2,512,256]{2,1,0:T(8,128)S(1)} custom-call(bf16[16,96,128]{2,1,0:T(8,128)(2,1)S(1)} %collective-permute-done.1.refs_0_, f32[2,512,256]{2,1,0:T(8,128)S(1)} %shard_map.40.refs_1_, bf16[512,4096]{1,0:T(8,128)(2,1)S(1)} %shard_map.38.refs_2_, bf16[512,4096]{1,0:T(8,128)(2,1)S(1)} %shard_map.39.refs_3_), custom_call_target="tpu_custom_call" | custom-call | flops 402653184 | bytes 3145728 | tf_op jit(solution)/shard_map/pallas_call | solution.py:130
  52.7 0.0 collective-permute-done.refs_0_
  52.7 1.0 %shard_map.42 = f32[384,512]{1,0:T(8,128)S(1)} custom-call(bf16[16,96,128]{2,1,0:T(8,128)(2,1)S(1)} %collective-permute-done.refs_0_, f32[2,512,256]{2,1,0:T(8,128)S(1)} %shard_map.41.refs_1_, bf16[512,4096]{1,0:T(8,128)(2,1)S(1)} %shard_map.38.refs_2_, bf16[512,4096]{1,0:T(8,128)(2,1)S(1)} %shard_map.39.refs_3_), custom_call_target="tpu_custom_call" | custom-call | flops 402653184 | bytes 3145728 | tf_op jit(solution)/shard_map/pallas_call | solution.py:147
  53.7 0.1 convert_element_type.12
  53.8 21.9 %all_to_all.19 = f16[16,24,512]{2,1,0:T(8,128)(2,1)S(1)} all-to-all(f16[16,24,512]{2,1,0:T(8,128)(2,1)S(1)} %bitcast.9), channel_id=1, replica_groups=mesh['z'=8,'x'=4,'c'=2,'y'=8] {'y','c'}, dimensions={0} | all-to-all | bytes 786432 | tf_op jit(solution)/shard_map/all_to_all | solution.py:174
  75.6 0.1 convert_reduce_fusion
  75.7 0.6 multiply_convert_fusion
Async XLA Ops:
  0.0 47.0 %collective-permute-start.4 = (bf16[512,4096]{1,0:T(8,128)(2,1)}, bf16[512,4096]{1,0:T(8,128)(2,1)S(1)}, u32[]{:S(2)}, u32[]{:S(2)}) collective-permute-start(bf16[512,4096]{1,0:T(8,128)(2,1)} %m_ref.1), channel_id=1, source_target_pairs={{0,8},{8,0},{1,9},{9,1},{2,10},{10,2},{3,11},{11,3},{4,12},{12,4},... | collective-permute-start | bytes 12582920 | tf_op jit(solution)/shard_map/ppermute | solution.py:163
  8.8 0.8 %copy-start.1 = (bf16[384,64]{0,1:T(8,128)(2,1)S(1)}, bf16[384,64]{0,1:T(8,128)(2,1)}, u32[]{:S(2)}) copy-start(bf16[384,64]{0,1:T(8,128)(2,1)} %param.3) | copy-start | bytes 147460
  29.2 19.6 %collective-permute-start.2 = (bf16[16,96,128]{2,1,0:T(8,128)(2,1)S(1)}, bf16[16,96,128]{2,1,0:T(8,128)(2,1)S(1)}, u32[]{:S(2)}, u32[]{:S(2)}) collective-permute-start(bf16[16,96,128]{2,1,0:T(8,128)(2,1)S(1)} %all_to_all.18.refs_0_), channel_id=1, source_target_pairs={{0,32},{16,48},{32,0},{48,16},{1,33},{17,49},{33,1},{49,17},{2,34}... | collective-permute-start | bytes 1179656 | tf_op jit(solution)/shard_map/ppermute | solution.py:167
  33.9 18.0 %collective-permute-start.1 = (bf16[16,96,128]{2,1,0:T(8,128)(2,1)S(1)}, bf16[16,96,128]{2,1,0:T(8,128)(2,1)S(1)}, u32[]{:S(2)}, u32[]{:S(2)}) collective-permute-start(bf16[16,96,128]{2,1,0:T(8,128)(2,1)S(1)} %all_to_all.18.refs_0_), channel_id=1, source_target_pairs={{0,16},{16,32},{32,48},{48,0},{1,17},{17,33},{33,49},{49,1},{2,18}... | collective-permute-start | bytes 1179656 | tf_op jit(solution)/shard_map/ppermute | solution.py:167
  36.1 16.6 %collective-permute-start = (bf16[16,96,128]{2,1,0:T(8,128)(2,1)S(1)}, bf16[16,96,128]{2,1,0:T(8,128)(2,1)S(1)}, u32[]{:S(2)}, u32[]{:S(2)}) collective-permute-start(bf16[16,96,128]{2,1,0:T(8,128)(2,1)S(1)} %all_to_all.18.refs_0_), channel_id=1, source_target_pairs={{0,48},{16,0},{32,16},{48,32},{1,49},{17,1},{33,17},{49,33},{2,50}... | collective-permute-start | bytes 1179656 | tf_op jit(solution)/shard_map/ppermute | solution.py:167
  40.4 6.6 %collective-permute-start.3 = (s32[4,32]{1,0:T(4,128)}, s32[4,32]{1,0:T(4,128)S(1)}, u32[]{:S(2)}, u32[]{:S(2)}) collective-permute-start(s32[4,32]{1,0:T(4,128)} %allowed_ref), channel_id=1, source_target_pairs={{0,8},{8,0},{1,9},{9,1},{2,10},{10,2},{3,11},{11,3},{4,12},{12,4},... | collective-permute-start | bytes 1544 | tf_op jit(solution)/shard_map/ppermute | solution.py:170
  42.4 2.2 %copy-start = (bf16[512,4096]{1,0:T(8,128)(2,1)S(1)}, bf16[512,4096]{1,0:T(8,128)(2,1)}, u32[]{:S(2)}) copy-start(bf16[512,4096]{1,0:T(8,128)(2,1)} %m_ref.1) | copy-start | bytes 12582916
  44.6 0.7 copy-start.2

commit v6 on v5

--- a/solution.py
+++ b/solution.py
@@ -89,20 +89,44 @@
     return lax.rem(lax.axis_index("x") + (NX - shift), NX)
 
 
-def some_kernel(shifts, *refs):
-    block_refs = refs[: len(shifts)]
-    own_ref, other_ref, acc_ref, w_ref = refs[-4:]
-    before_ref = refs[len(shifts)] if len(refs) > len(shifts) + 4 else None
-    for n, shift in enumerate(shifts):
-        spread(block_refs[n], w_ref)
-        w = w_ref[...]
-        for i, m_ref in enumerate((own_ref, other_ref)):
-            part = block_dot(m_ref, w, source(shift))
-            if n > 0:
-                part += acc_ref[i]
-            elif before_ref is not None:
-                part += before_ref[i]
-            acc_ref[i] = part
+def load_kernel(m_ref, after_ref, out_ref, sem):
+    del after_ref
+    copy = pltpu.make_async_copy(m_ref, out_ref, sem)
+    copy.start()
+    copy.wait()
+
+
+def load(m, after):
+    return pl.pallas_call(
+        load_kernel,
+        in_specs=[pl.BlockSpec(memory_space=pl.ANY)] * 2,
+        out_specs=pl.BlockSpec(memory_space=pltpu.VMEM),
+        out_shape=jax.ShapeDtypeStruct((ROWS, COLS), jnp.bfloat16),
+        scratch_shapes=[pltpu.SemaphoreType.DMA],
+        compiler_params=pltpu.CompilerParams(vmem_limit_bytes=48 << 20),
+        cost_estimate=pl.CostEstimate(flops=0, bytes_accessed=4 * ROWS * COLS, transcendentals=0),
+    )(m, after)
+
+
+def own_kernel(block_ref, own_ref, acc_ref, w_ref):
+    spread(block_ref, w_ref)
+    acc_ref[...] = block_dot(own_ref, w_ref[...], source(0))
+
+
+def two_kernel(block_ref, far_ref, acc_own_ref, own_ref, other_ref, acc_ref, w_ref):
+    spread(block_ref, w_ref)
+    acc_ref[1] = block_dot(other_ref, w_ref[...], source(0))
+    spread(far_ref, w_ref)
+    w = w_ref[...]
+    acc_ref[0] = acc_own_ref[...] + block_dot(own_ref, w, source(2))
+    acc_ref[1] += block_dot(other_ref, w, source(2))
+
+
+def next_kernel(block_ref, in_ref, own_ref, other_ref, acc_ref, w_ref):
+    spread(block_ref, w_ref)
+    w = w_ref[...]
+    for i, m_ref in enumerate((own_ref, other_ref)):
+        acc_ref[i] = in_ref[i] + block_dot(m_ref, w, source(1))
 
 
 def last_kernel(shift, block_ref, in_ref, own_ref, other_ref, out_ref, w_ref, acc_ref):
@@ -123,21 +147,16 @@
 WIDE = NZ * NC * 64
 
 
-def some_dots(shifts, blocks, before, own, other):
-    def some(*refs):
-        some_kernel(shifts, *refs)
-
-    return pl.pallas_call(
-        some,
-        in_specs=[pl.BlockSpec(memory_space=pltpu.VMEM)] * (len(shifts) + len(before) + 2),
-        out_specs=pl.BlockSpec(memory_space=pltpu.VMEM),
-        out_shape=jax.ShapeDtypeStruct(ACC, jnp.float32),
+def some_dots(kernel, shape, flops, *args):
+    return pl.pallas_call(
+        kernel,
+        in_specs=[pl.BlockSpec(memory_space=pltpu.VMEM)] * len(args),
+        out_specs=pl.BlockSpec(memory_space=pltpu.VMEM),
+        out_shape=jax.ShapeDtypeStruct(shape, jnp.float32),
         scratch_shapes=[pltpu.VMEM((WIDE, 256), jnp.bfloat16)],
         compiler_params=pltpu.CompilerParams(vmem_limit_bytes=16 << 20),
-        cost_estimate=pl.CostEstimate(
-            flops=len(shifts) * OP * ROWS * COLS // 2, bytes_accessed=3 << 20, transcendentals=0
-        ),
-    )(*blocks, *before, own, other)
+        cost_estimate=pl.CostEstimate(flops=flops, bytes_accessed=3 << 20, transcendentals=0),
+    )(*args)
 
 
 def last_dots(shift, block, acc, own, other):
@@ -156,20 +175,22 @@
 
 
 SHIFTS = (2, 1, 3)
+HIDE = 1 << 36
 
 
 def shards(amplitudes, integrals, allowed):
     swap = [(0, 1), (1, 0)]
-    raw = lax.ppermute(integrals, "c", swap)
     pieces = pack(amplitudes.T)
+    pieces, allowed = lax.optimization_barrier((pieces, allowed))
     over_z = lax.all_to_all(pieces.reshape(NZ * NC * 96, 128), ("z", "c"), 0, 0, tiled=True)
+    own = mask(allowed, integrals)
+    other = lax.ppermute(own, "c", swap)
     block = over_z.reshape(NZ * NC, 96, 128)
     far, right, left = [lax.ppermute(block, "x", [(i, (i + d) % NX) for i in range(NX)]) for d in SHIFTS]
-    block, allowed = lax.optimization_barrier((block, allowed))
-    own = mask(allowed, integrals)
-    other = mask(lax.ppermute(allowed, "c", swap), raw)
-    acc = some_dots((0, 2), (block, far), (), own, other)
-    acc = some_dots((1,), (right,), (acc,), own, other)
+    acc = some_dots(own_kernel, ACC[1:], HIDE, block, own)
+    own, other = load(own, acc), load(other, acc)
+    acc = some_dots(two_kernel, ACC, OP * ROWS * COLS, block, far, acc, own, other)
+    acc = some_dots(next_kernel, ACC, OP * ROWS * COLS // 2, right, acc, own, other)
     partial_sums = last_dots(3, left, acc, own, other).astype(jnp.float16)
     landed = lax.all_to_all(partial_sums, ("y", "c"), 0, 0, tiled=True)
     total = jnp.sum(landed.reshape(NY, 2 * SEG, ROWS).astype(jnp.float32), axis=0)

time: 76.7 us -> 75.9 us (0.990)
  blocking collectives: 41.3 us -> 21.9 us
  Pallas kernels: 6.98 us -> 14.8 us
  waiting for transfers between devices: 1.64 us -> 9.16 us
  starting transfers between devices: 21.9 us -> 25 us
    all_to_all x1 -> x0, blocking collectives: 19.4 us -> none  [shards(): lax.all_to_all(pieces.reshape(NZ * NC * 96, 128), ('z', 'c'), 0, 0, tiled...]
    all_to_all x0 -> x1, starting transfers between devices: none -> 11.8 us  [shards(): lax.all_to_all(pieces.reshape(NZ * NC * 96, 128), ('z', 'c'), 0, 0, tiled...]
    ppermute x2 -> x1, starting transfers between devices: 10.8 us -> 2 us  [shards(): other = lax.ppermute(own, 'c', swap)]
    pallas_call x2 -> x5, Pallas kernels: 2.25 us -> 9.08 us  [the longest x3 4.69 us: some_dots(): pl.pallas_call(kernel, in_specs=[pl.BlockSpec(memory_space=pltpu.VMEM)] *...]
    all_to_all x0 -> x1, waiting for transfers between devices: none -> 5.97 us  [shards(): lax.all_to_all(pieces.reshape(NZ * NC * 96, 128), ('z', 'c'), 0, 0, tiled...]
    ppermute x3, waiting for transfers between devices: 1.64 us -> 3.18 us  [shards(): lax.ppermute(block, 'x', [(i, (i + d) % NX) for i in range(NX)])]
    pallas_call x1, Pallas kernels: 0.22 us -> 1.02 us  [pack(): pl.pallas_call(pack_kernel, out_shape=jax.ShapeDtypeStruct((NZ, NC, 96, 1...]
    pallas_call x2 -> x1, Pallas kernels: 3.5 us -> 3.7 us  [mask(): pl.pallas_call(mask_kernel, in_specs=[pl.BlockSpec(memory_space=pltpu.SME...]
  transfers between devices with their start and end apart: 5 -> 5, of which waited for: 1 -> 2; matrix products, arithmetic and copies ran while one was open for 0% -> 0% of each run, Pallas kernels for 8% -> 17%
where the time goes in v6:
time: 75.9 us; the launch traced here: 75.3 us
  starting transfers between devices  25 us (33%)
  blocking collectives  21.9 us (29%)
  Pallas kernels  14.8 us (19%)
  waiting for transfers between devices  9.16 us (12%)
  local copies, waits for them, and re-layouts  3.66 us (5%)
    all_to_all x1, blocking collectives, shards(): landed = lax.all_to_all(partial_sums, ('y', 'c'), 0, 0, tiled=True)  21.9 us
    all_to_all x1, starting transfers between devices, shards(): lax.all_to_all(pieces.reshape(NZ * NC * 96, 128), ('z', 'c'), 0, 0, tiled...  11.8 us
    ppermute x3, starting transfers between devices, shards(): lax.ppermute(block, 'x', [(i, (i + d) % NX) for i in range(NX)])  11.1 us
    all_to_all x1, waiting for transfers between devices, shards(): lax.all_to_all(pieces.reshape(NZ * NC * 96, 128), ('z', 'c'), 0, 0, tiled...  5.97 us
    pallas_call x3, Pallas kernels, some_dots(): pl.pallas_call(kernel, in_specs=[pl.BlockSpec(memory_space=pltpu.VMEM)] *...  4.69 us
    pallas_call x2, Pallas kernels, load(): pl.pallas_call(load_kernel, in_specs=[pl.BlockSpec(memory_space=pl.ANY)]...  4.4 us
    pallas_call x1, Pallas kernels, mask(): pl.pallas_call(mask_kernel, in_specs=[pl.BlockSpec(memory_space=pltpu.SME...  3.7 us
    unnamed x6, local copies, waits for them, and re-layouts  3.66 us
  transfers between devices with their start and end apart: 5, of which 2 were waited for; matrix products, arithmetic and copies ran while one was open for 0% of the time, Pallas kernels for 17%

profile of v6, /device:TPU:1, one launch (start us, length us, event | category | flops | bytes accessed | tf_op | source)
XLA Modules:
  0.0 75.3 jit_solution(1823823611227857225)
XLA Ops:
  0.0 0.0 copy-start.1
  0.0 0.8 %copy-done.1 = bf16[384,64]{0,1:T(8,128)(2,1)S(1)} copy-done((bf16[384,64]{0,1:T(8,128)(2,1)S(1)}, bf16[384,64]{0,1:T(8,128)(2,1)}, u32[]{:S(2)}) %copy-start.1) | copy-done | bytes 49176
  0.8 1.0 %shard_map.37 = bf16[8,2,96,128]{3,2,1,0:T(8,128)(2,1)} custom-call(bf16[64,384]{1,0:T(8,128)(2,1)S(1)} %bitcast.7), custom_call_target="tpu_custom_call" | custom-call | flops 25165824 | bytes 450000 | tf_op jit(solution)/shard_map/pallas_call | solution.py:41
  1.8 11.8 %all-to-all-start = ((bf16[16,96,128]{2,1,0:T(8,128)(2,1)}), bf16[16,96,128]{2,1,0:T(8,128)(2,1)S(1)}, u32[]{:S(2)}, u32[]{:S(2)}) async-start(bf16[16,96,128]{2,1,0:T(8,128)(2,1)} %bitcast.1), calls=%async_computation | async-start | bytes 786432 | tf_op jit(solution)/shard_map/all_to_all | solution.py:185
  13.7 0.0 copy-start
  13.7 2.2 %copy-done = bf16[512,4096]{1,0:T(8,128)(2,1)S(1)} copy-done((bf16[512,4096]{1,0:T(8,128)(2,1)S(1)}, bf16[512,4096]{1,0:T(8,128)(2,1)}, u32[]{:S(2)}) %copy-start) | copy-done | bytes 4194328
  15.8 0.0 copy-start.2
  15.8 0.7 copy-done.2
  16.5 3.7 %shard_map.38.own_ref.m_ref = bf16[512,4096]{1,0:T(8,128)(2,1)} custom-call(s32[4,32]{1,0:T(4,128)S(1)} %copy-done.2, bf16[512,4096]{1,0:T(8,128)(2,1)S(1)} %copy-done), custom_call_target="tpu_custom_call" | custom-call | flops 2097152 | bytes 8388608 | tf_op jit(solution)/shard_map/pallas_call | solution.py:63
  20.2 2.0 %collective-permute-start.3 = (bf16[512,4096]{1,0:T(8,128)(2,1)}, bf16[512,4096]{1,0:T(8,128)(2,1)}, u32[]{:S(2)}, u32[]{:S(2)}) collective-permute-start(bf16[512,4096]{1,0:T(8,128)(2,1)} %shard_map.38.own_ref.m_ref), channel_id=1, source_target_pairs={{0,8},{8,0},{1,9},{9,1},{2,10},{10,2},{3,11},{11,3},{4,12},{12,4},... | collective-permute-start | bytes 12582920 | tf_op jit(solution)/shard_map/ppermute | solution.py:187
  22.2 6.0 %all-to-all-done.block_ref = bf16[16,96,128]{2,1,0:T(8,128)(2,1)S(1)} async-done(((bf16[16,96,128]{2,1,0:T(8,128)(2,1)}), bf16[16,96,128]{2,1,0:T(8,128)(2,1)S(1)}, u32[]{:S(2)}, u32[]{:S(2)}) %all-to-all-start) | async-done | bytes 393248 | tf_op jit(solution)/shard_map/all_to_all | solution.py:185
  28.2 4.6 %collective-permute-start.2 = (bf16[16,96,128]{2,1,0:T(8,128)(2,1)S(1)}, bf16[16,96,128]{2,1,0:T(8,128)(2,1)S(1)}, u32[]{:S(2)}, u32[]{:S(2)}) collective-permute-start(bf16[16,96,128]{2,1,0:T(8,128)(2,1)S(1)} %all-to-all-done.block_ref), channel_id=1, source_target_pairs={{0,32},{16,48},{32,0},{48,16},{1,33},{17,49},{33,1},{49,17},{2,34}... | collective-permute-start | bytes 1179656 | tf_op jit(solution)/shard_map/ppermute | solution.py:189
  32.9 2.2 %collective-permute-start.1 = (bf16[16,96,128]{2,1,0:T(8,128)(2,1)S(1)}, bf16[16,96,128]{2,1,0:T(8,128)(2,1)S(1)}, u32[]{:S(2)}, u32[]{:S(2)}) collective-permute-start(bf16[16,96,128]{2,1,0:T(8,128)(2,1)S(1)} %all-to-all-done.block_ref), channel_id=1, source_target_pairs={{0,16},{16,32},{32,48},{48,0},{1,17},{17,33},{33,49},{49,1},{2,18}... | collective-permute-start | bytes 1179656 | tf_op jit(solution)/shard_map/ppermute | solution.py:189
  35.1 4.3 %collective-permute-start = (bf16[16,96,128]{2,1,0:T(8,128)(2,1)S(1)}, bf16[16,96,128]{2,1,0:T(8,128)(2,1)S(1)}, u32[]{:S(2)}, u32[]{:S(2)}) collective-permute-start(bf16[16,96,128]{2,1,0:T(8,128)(2,1)S(1)} %all-to-all-done.block_ref), channel_id=1, source_target_pairs={{0,48},{16,0},{32,16},{48,32},{1,49},{17,1},{33,17},{49,33},{2,50}... | collective-permute-start | bytes 1179656 | tf_op jit(solution)/shard_map/ppermute | solution.py:189
  39.4 2.7 %shard_map.39.after_ref.acc_own_ref = f32[512,256]{1,0:T(8,128)S(1)} custom-call(bf16[16,96,128]{2,1,0:T(8,128)(2,1)S(1)} %all-to-all-done.block_ref, bf16[512,4096]{1,0:T(8,128)(2,1)} %shard_map.38.own_ref.m_ref), custom_call_target="tpu_custom_call" | custom-call | flops 68719476736 | bytes 3145728 | tf_op jit(solution)/shard_map/pallas_call | solution.py:151
  42.1 2.2 %shard_map.40.own_ref.refs_2_ = bf16[512,4096]{1,0:T(8,128)(2,1)S(1)} custom-call(bf16[512,4096]{1,0:T(8,128)(2,1)} %shard_map.38.own_ref.m_ref, f32[512,256]{1,0:T(8,128)S(1)} %shard_map.39.after_ref.acc_own_ref), custom_call_target="tpu_custom_call" | custom-call | bytes 8388608 | tf_op jit(solution)/shard_map/pallas_call | solution.py:100
  44.3 0.0 collective-permute-done.3.m_ref
  44.3 2.2 %shard_map.41.other_ref.refs_3_ = bf16[512,4096]{1,0:T(8,128)(2,1)S(1)} custom-call(bf16[512,4096]{1,0:T(8,128)(2,1)} %collective-permute-done.3.m_ref, f32[512,256]{1,0:T(8,128)S(1)} %shard_map.39.after_ref.acc_own_ref), custom_call_target="tpu_custom_call" | custom-call | bytes 8388608 | tf_op jit(solution)/shard_map/pallas_call | solution.py:100
  46.5 0.0 collective-permute-done.2.far_ref
  46.5 1.1 %shard_map.42.in_ref = f32[2,512,256]{2,1,0:T(8,128)S(1)} custom-call(bf16[16,96,128]{2,1,0:T(8,128)(2,1)S(1)} %all-to-all-done.block_ref, bf16[16,96,128]{2,1,0:T(8,128)(2,1)S(1)} %collective-permute-done.2.far_ref, f32[512,256]{1,0:T(8,128)S(1)} %shard_map.39.after_ref.acc_own_ref, bf16[512,4096]{1,0:T(8,128)(2,1)S(1)} %shard_map.40.own_ref.refs_2_, ...), custom_call_target="tpu_custom_call" | custom-call | flops 805306368 | bytes 3145728 | tf_op jit(solution)/shard_map/pallas_call | solution.py:151
  47.7 3.2 %collective-permute-done.1.block_ref = bf16[16,96,128]{2,1,0:T(8,128)(2,1)S(1)} collective-permute-done((bf16[16,96,128]{2,1,0:T(8,128)(2,1)S(1)}, bf16[16,96,128]{2,1,0:T(8,128)(2,1)S(1)}, u32[]{:S(2)}, u32[]{:S(2)}) %collective-permute-start.1) | collective-permute-done | bytes 393248 | tf_op jit(solution)/shard_map/ppermute | solution.py:189
  50.8 0.8 %shard_map.43.refs_1_ = f32[2,512,256]{2,1,0:T(8,128)S(1)} custom-call(bf16[16,96,128]{2,1,0:T(8,128)(2,1)S(1)} %collective-permute-done.1.block_ref, f32[2,512,256]{2,1,0:T(8,128)S(1)} %shard_map.42.in_ref, bf16[512,4096]{1,0:T(8,128)(2,1)S(1)} %shard_map.40.own_ref.refs_2_, bf16[512,4096]{1,0:T(8,128)(2,1)S(1)} %shard_map.41.other_ref.refs_3_), custom_call_target="tpu_custom_call" | custom-call | flops 402653184 | bytes 3145728 | tf_op jit(solution)/shard_map/pallas_call | solution.py:151
  51.7 0.0 collective-permute-done.refs_0_
  51.7 1.0 %shard_map.44 = f32[384,512]{1,0:T(8,128)S(1)} custom-call(bf16[16,96,128]{2,1,0:T(8,128)(2,1)S(1)} %collective-permute-done.refs_0_, f32[2,512,256]{2,1,0:T(8,128)S(1)} %shard_map.43.refs_1_, bf16[512,4096]{1,0:T(8,128)(2,1)S(1)} %shard_map.40.own_ref.refs_2_, bf16[512,4096]{1,0:T(8,128)(2,1)S(1)} %shard_map.41.other_ref.refs_3_), custom_call_target="tpu_custom_call" | custom-call | flops 402653184 | bytes 3145728 | tf_op jit(solution)/shard_map/pallas_call | solution.py:166
  52.7 0.1 convert_element_type.12
  52.8 21.9 %all_to_all.18 = f16[16,24,512]{2,1,0:T(8,128)(2,1)S(1)} all-to-all(f16[16,24,512]{2,1,0:T(8,128)(2,1)S(1)} %bitcast.8), channel_id=1, replica_groups=mesh['z'=8,'x'=4,'c'=2,'y'=8] {'y','c'}, dimensions={0} | all-to-all | bytes 786432 | tf_op jit(solution)/shard_map/all_to_all | solution.py:195
  74.6 0.1 convert_reduce_fusion
  74.7 0.6 multiply_convert_fusion
Async XLA Ops:
  0.0 0.8 %copy-start.1 = (bf16[384,64]{0,1:T(8,128)(2,1)S(1)}, bf16[384,64]{0,1:T(8,128)(2,1)}, u32[]{:S(2)}) copy-start(bf16[384,64]{0,1:T(8,128)(2,1)} %param.3) | copy-start | bytes 147460
  1.8 26.4 %all-to-all-start = ((bf16[16,96,128]{2,1,0:T(8,128)(2,1)}), bf16[16,96,128]{2,1,0:T(8,128)(2,1)S(1)}, u32[]{:S(2)}, u32[]{:S(2)}) async-start(bf16[16,96,128]{2,1,0:T(8,128)(2,1)} %bitcast.1), calls=%async_computation | async-start | bytes 786432 | tf_op jit(solution)/shard_map/all_to_all | solution.py:185
  13.7 2.2 %copy-start = (bf16[512,4096]{1,0:T(8,128)(2,1)S(1)}, bf16[512,4096]{1,0:T(8,128)(2,1)}, u32[]{:S(2)}) copy-start(bf16[512,4096]{1,0:T(8,128)(2,1)} %m_ref.1) | copy-start | bytes 12582916
  15.8 0.7 copy-start.2
  20.2 24.1 %collective-permute-start.3 = (bf16[512,4096]{1,0:T(8,128)(2,1)}, bf16[512,4096]{1,0:T(8,128)(2,1)}, u32[]{:S(2)}, u32[]{:S(2)}) collective-permute-start(bf16[512,4096]{1,0:T(8,128)(2,1)} %shard_map.38.own_ref.m_ref), channel_id=1, source_target_pairs={{0,8},{8,0},{1,9},{9,1},{2,10},{10,2},{3,11},{11,3},{4,12},{12,4},... | collective-permute-start | bytes 12582920 | tf_op jit(solution)/shard_map/ppermute | solution.py:187
  28.2 18.3 %collective-permute-start.2 = (bf16[16,96,128]{2,1,0:T(8,128)(2,1)S(1)}, bf16[16,96,128]{2,1,0:T(8,128)(2,1)S(1)}, u32[]{:S(2)}, u32[]{:S(2)}) collective-permute-start(bf16[16,96,128]{2,1,0:T(8,128)(2,1)S(1)} %all-to-all-done.block_ref), channel_id=1, source_target_pairs={{0,32},{16,48},{32,0},{48,16},{1,33},{17,49},{33,1},{49,17},{2,34}... | collective-permute-start | bytes 1179656 | tf_op jit(solution)/shard_map/ppermute | solution.py:189
  32.9 18.0 %collective-permute-start.1 = (bf16[16,96,128]{2,1,0:T(8,128)(2,1)S(1)}, bf16[16,96,128]{2,1,0:T(8,128)(2,1)S(1)}, u32[]{:S(2)}, u32[]{:S(2)}) collective-permute-start(bf16[16,96,128]{2,1,0:T(8,128)(2,1)S(1)} %all-to-all-done.block_ref), channel_id=1, source_target_pairs={{0,16},{16,32},{32,48},{48,0},{1,17},{17,33},{33,49},{49,1},{2,18}... | collective-permute-start | bytes 1179656 | tf_op jit(solution)/shard_map/ppermute | solution.py:189
  35.1 16.6 %collective-permute-start = (bf16[16,96,128]{2,1,0:T(8,128)(2,1)S(1)}, bf16[16,96,128]{2,1,0:T(8,128)(2,1)S(1)}, u32[]{:S(2)}, u32[]{:S(2)}) collective-permute-start(bf16[16,96,128]{2,1,0:T(8,128)(2,1)S(1)} %all-to-all-done.block_ref), channel_id=1, source_target_pairs={{0,48},{16,0},{32,16},{48,32},{1,49},{17,1},{33,17},{49,33},{2,50}... | collective-permute-start | bytes 1179656 | tf_op jit(solution)/shard_map/ppermute | solution.py:189

commit v7 on v6

--- a/solution.py
+++ b/solution.py
@@ -33,14 +33,14 @@
         both = picked[:, 256 + core * 128 : 256 + (core + 1) * 128]
         tail = jnp.where(low, both[:32], both[32:]).astype(jnp.bfloat16)
         for z in range(NZ):
-            out_ref[z, core, :64] = head
-            out_ref[z, core, 64:] = tail
+            out_ref[core, z, :64] = head
+            out_ref[core, z, 64:] = tail
 
 
 def pack(a):
     return pl.pallas_call(
         pack_kernel,
-        out_shape=jax.ShapeDtypeStruct((NZ, NC, 96, 128), jnp.bfloat16),
+        out_shape=jax.ShapeDtypeStruct((NC, NZ, 96, 128), jnp.bfloat16),
         in_specs=[pl.BlockSpec(memory_space=pltpu.VMEM)],
         out_specs=pl.BlockSpec(memory_space=pltpu.VMEM),
         compiler_params=pltpu.CompilerParams(vmem_limit_bytes=4 << 20),
@@ -72,7 +72,7 @@
 
 def spread(block_ref, w_ref):
     for zc in range(NZ * NC):
-        at = zc * 64
+        at = (zc % NZ * NC + zc // NZ) * 64
         w_ref[at : at + 64, :128] = block_ref[zc, :64]
         tail = block_ref[zc, 64:]
         w_ref[at : at + 32, 128:] = tail
@@ -139,7 +139,7 @@
     sums = jnp.where(leads, own, other), jnp.where(leads, other, own)
     for y in range(NY):
         for c in range(NC):
-            at = (y * NC + c) * SEG
+            at = (c * NY + y) * SEG
             out_ref[at : at + SEG] = sums[c][y * SEG : (y + 1) * SEG]
 
 
@@ -182,7 +182,7 @@
     swap = [(0, 1), (1, 0)]
     pieces = pack(amplitudes.T)
     pieces, allowed = lax.optimization_barrier((pieces, allowed))
-    over_z = lax.all_to_all(pieces.reshape(NZ * NC * 96, 128), ("z", "c"), 0, 0, tiled=True)
+    over_z = lax.all_to_all(pieces.reshape(NZ * NC * 96, 128), ("c", "z"), 0, 0, tiled=True)
     own = mask(allowed, integrals)
     other = lax.ppermute(own, "c", swap)
     block = over_z.reshape(NZ * NC, 96, 128)
@@ -192,8 +192,8 @@
     acc = some_dots(two_kernel, ACC, OP * ROWS * COLS, block, far, acc, own, other)
     acc = some_dots(next_kernel, ACC, OP * ROWS * COLS // 2, right, acc, own, other)
     partial_sums = last_dots(3, left, acc, own, other).astype(jnp.float16)
-    landed = lax.all_to_all(partial_sums, ("y", "c"), 0, 0, tiled=True)
-    total = jnp.sum(landed.reshape(NY, 2 * SEG, ROWS).astype(jnp.float32), axis=0)
+    landed = lax.all_to_all(partial_sums, ("c", "y"), 0, 0, tiled=True)
+    total = jnp.sum(landed.reshape(NC, NY, SEG, ROWS).astype(jnp.float32), axis=1).reshape(NC * SEG, ROWS)
     return (total * (1.0 / SCALE)).astype(jnp.bfloat16)
 
 

time: 75.9 us -> 72.2 us (0.951)
  blocking collectives: 21.9 us -> 19.8 us
  waiting for transfers between devices: 9.16 us -> 7.26 us
    all_to_all x1, waiting for transfers between devices: 5.97 us -> 3.87 us  [shards(): lax.all_to_all(pieces.reshape(NZ * NC * 96, 128), ('c', 'z'), 0, 0, tiled...]
    all_to_all x1, blocking collectives: 21.9 us -> 19.8 us  [shards(): landed = lax.all_to_all(partial_sums, ('c', 'y'), 0, 0, tiled=True)]
  transfers between devices with their start and end apart: 5 -> 5, of which waited for: 2 -> 2; matrix products, arithmetic and copies ran while one was open for 0% -> 0% of each run, Pallas kernels for 17% -> 18%
where the time goes in v7:
time: 72.2 us; the launch traced here: 71.4 us
  starting transfers between devices  25 us (35%)
  blocking collectives  19.8 us (27%)
  Pallas kernels  14.8 us (20%)
  waiting for transfers between devices  7.26 us (10%)
  local copies, waits for them, and re-layouts  3.66 us (5%)
  other arithmetic  0.74 us (1%)
    all_to_all x1, blocking collectives, shards(): landed = lax.all_to_all(partial_sums, ('c', 'y'), 0, 0, tiled=True)  19.8 us
    all_to_all x1, starting transfers between devices, shards(): lax.all_to_all(pieces.reshape(NZ * NC * 96, 128), ('c', 'z'), 0, 0, tiled...  11.8 us
    ppermute x3, starting transfers between devices, shards(): lax.ppermute(block, 'x', [(i, (i + d) % NX) for i in range(NX)])  11.1 us
    pallas_call x3, Pallas kernels, some_dots(): pl.pallas_call(kernel, in_specs=[pl.BlockSpec(memory_space=pltpu.VMEM)] *...  4.68 us
    pallas_call x2, Pallas kernels, load(): pl.pallas_call(load_kernel, in_specs=[pl.BlockSpec(memory_space=pl.ANY)]...  4.4 us
    all_to_all x1, waiting for transfers between devices, shards(): lax.all_to_all(pieces.reshape(NZ * NC * 96, 128), ('c', 'z'), 0, 0, tiled...  3.87 us
    pallas_call x1, Pallas kernels, mask(): pl.pallas_call(mask_kernel, in_specs=[pl.BlockSpec(memory_space=pltpu.SME...  3.7 us
    unnamed x6, local copies, waits for them, and re-layouts  3.66 us
  transfers between devices with their start and end apart: 5, of which 2 were waited for; matrix products, arithmetic and copies ran while one was open for 0% of the time, Pallas kernels for 18%

profile of v7, /device:TPU:1, one launch (start us, length us, event | category | flops | bytes accessed | tf_op | source)
XLA Modules:
  0.0 71.4 jit_solution(6945909221854226295)
XLA Ops:
  0.0 0.0 copy-start.1
  0.0 0.8 %copy-done.1 = bf16[384,64]{0,1:T(8,128)(2,1)S(1)} copy-done((bf16[384,64]{0,1:T(8,128)(2,1)S(1)}, bf16[384,64]{0,1:T(8,128)(2,1)}, u32[]{:S(2)}) %copy-start.1) | copy-done | bytes 49176
  0.8 1.0 %shard_map.37 = bf16[2,8,96,128]{3,2,1,0:T(8,128)(2,1)} custom-call(bf16[64,384]{1,0:T(8,128)(2,1)S(1)} %bitcast.7), custom_call_target="tpu_custom_call" | custom-call | flops 25165824 | bytes 450000 | tf_op jit(solution)/shard_map/pallas_call | solution.py:41
  1.8 11.8 %all-to-all-start = ((bf16[16,96,128]{2,1,0:T(8,128)(2,1)}), bf16[16,96,128]{2,1,0:T(8,128)(2,1)S(1)}, u32[]{:S(2)}, u32[]{:S(2)}) async-start(bf16[16,96,128]{2,1,0:T(8,128)(2,1)} %bitcast.1), calls=%async_computation | async-start | bytes 786432 | tf_op jit(solution)/shard_map/all_to_all | solution.py:185
  13.7 0.0 copy-start
  13.7 2.2 %copy-done = bf16[512,4096]{1,0:T(8,128)(2,1)S(1)} copy-done((bf16[512,4096]{1,0:T(8,128)(2,1)S(1)}, bf16[512,4096]{1,0:T(8,128)(2,1)}, u32[]{:S(2)}) %copy-start) | copy-done | bytes 4194328
  15.8 0.0 copy-start.2
  15.8 0.7 copy-done.2
  16.5 3.7 %shard_map.38.own_ref.m_ref = bf16[512,4096]{1,0:T(8,128)(2,1)} custom-call(s32[4,32]{1,0:T(4,128)S(1)} %copy-done.2, bf16[512,4096]{1,0:T(8,128)(2,1)S(1)} %copy-done), custom_call_target="tpu_custom_call" | custom-call | flops 2097152 | bytes 8388608 | tf_op jit(solution)/shard_map/pallas_call | solution.py:63
  20.2 2.0 %collective-permute-start.3 = (bf16[512,4096]{1,0:T(8,128)(2,1)}, bf16[512,4096]{1,0:T(8,128)(2,1)}, u32[]{:S(2)}, u32[]{:S(2)}) collective-permute-start(bf16[512,4096]{1,0:T(8,128)(2,1)} %shard_map.38.own_ref.m_ref), channel_id=1, source_target_pairs={{0,8},{8,0},{1,9},{9,1},{2,10},{10,2},{3,11},{11,3},{4,12},{12,4},... | collective-permute-start | bytes 12582920 | tf_op jit(solution)/shard_map/ppermute | solution.py:187
  22.2 3.9 %all-to-all-done.block_ref = bf16[16,96,128]{2,1,0:T(8,128)(2,1)S(1)} async-done(((bf16[16,96,128]{2,1,0:T(8,128)(2,1)}), bf16[16,96,128]{2,1,0:T(8,128)(2,1)S(1)}, u32[]{:S(2)}, u32[]{:S(2)}) %all-to-all-start) | async-done | bytes 393248 | tf_op jit(solution)/shard_map/all_to_all | solution.py:185
  26.1 4.6 %collective-permute-start.2 = (bf16[16,96,128]{2,1,0:T(8,128)(2,1)S(1)}, bf16[16,96,128]{2,1,0:T(8,128)(2,1)S(1)}, u32[]{:S(2)}, u32[]{:S(2)}) collective-permute-start(bf16[16,96,128]{2,1,0:T(8,128)(2,1)S(1)} %all-to-all-done.block_ref), channel_id=1, source_target_pairs={{0,32},{16,48},{32,0},{48,16},{1,33},{17,49},{33,1},{49,17},{2,34}... | collective-permute-start | bytes 1179656 | tf_op jit(solution)/shard_map/ppermute | solution.py:189
  30.7 2.2 %collective-permute-start.1 = (bf16[16,96,128]{2,1,0:T(8,128)(2,1)S(1)}, bf16[16,96,128]{2,1,0:T(8,128)(2,1)S(1)}, u32[]{:S(2)}, u32[]{:S(2)}) collective-permute-start(bf16[16,96,128]{2,1,0:T(8,128)(2,1)S(1)} %all-to-all-done.block_ref), channel_id=1, source_target_pairs={{0,16},{16,32},{32,48},{48,0},{1,17},{17,33},{33,49},{49,1},{2,18}... | collective-permute-start | bytes 1179656 | tf_op jit(solution)/shard_map/ppermute | solution.py:189
  33.0 4.3 %collective-permute-start = (bf16[16,96,128]{2,1,0:T(8,128)(2,1)S(1)}, bf16[16,96,128]{2,1,0:T(8,128)(2,1)S(1)}, u32[]{:S(2)}, u32[]{:S(2)}) collective-permute-start(bf16[16,96,128]{2,1,0:T(8,128)(2,1)S(1)} %all-to-all-done.block_ref), channel_id=1, source_target_pairs={{0,48},{16,0},{32,16},{48,32},{1,49},{17,1},{33,17},{49,33},{2,50}... | collective-permute-start | bytes 1179656 | tf_op jit(solution)/shard_map/ppermute | solution.py:189
  37.2 2.7 %shard_map.39.after_ref.acc_own_ref = f32[512,256]{1,0:T(8,128)S(1)} custom-call(bf16[16,96,128]{2,1,0:T(8,128)(2,1)S(1)} %all-to-all-done.block_ref, bf16[512,4096]{1,0:T(8,128)(2,1)} %shard_map.38.own_ref.m_ref), custom_call_target="tpu_custom_call" | custom-call | flops 68719476736 | bytes 3145728 | tf_op jit(solution)/shard_map/pallas_call | solution.py:151
  40.0 2.2 %shard_map.40.own_ref.refs_2_ = bf16[512,4096]{1,0:T(8,128)(2,1)S(1)} custom-call(bf16[512,4096]{1,0:T(8,128)(2,1)} %shard_map.38.own_ref.m_ref, f32[512,256]{1,0:T(8,128)S(1)} %shard_map.39.after_ref.acc_own_ref), custom_call_target="tpu_custom_call" | custom-call | bytes 8388608 | tf_op jit(solution)/shard_map/pallas_call | solution.py:100
  42.2 0.0 collective-permute-done.3.m_ref
  42.2 2.2 %shard_map.41.other_ref.refs_3_ = bf16[512,4096]{1,0:T(8,128)(2,1)S(1)} custom-call(bf16[512,4096]{1,0:T(8,128)(2,1)} %collective-permute-done.3.m_ref, f32[512,256]{1,0:T(8,128)S(1)} %shard_map.39.after_ref.acc_own_ref), custom_call_target="tpu_custom_call" | custom-call | bytes 8388608 | tf_op jit(solution)/shard_map/pallas_call | solution.py:100
  44.4 0.0 collective-permute-done.2.far_ref
  44.4 1.1 %shard_map.42.in_ref = f32[2,512,256]{2,1,0:T(8,128)S(1)} custom-call(bf16[16,96,128]{2,1,0:T(8,128)(2,1)S(1)} %all-to-all-done.block_ref, bf16[16,96,128]{2,1,0:T(8,128)(2,1)S(1)} %collective-permute-done.2.far_ref, f32[512,256]{1,0:T(8,128)S(1)} %shard_map.39.after_ref.acc_own_ref, bf16[512,4096]{1,0:T(8,128)(2,1)S(1)} %shard_map.40.own_ref.refs_2_, ...), custom_call_target="tpu_custom_call" | custom-call | flops 805306368 | bytes 3145728 | tf_op jit(solution)/shard_map/pallas_call | solution.py:151
  45.6 3.4 %collective-permute-done.1.block_ref = bf16[16,96,128]{2,1,0:T(8,128)(2,1)S(1)} collective-permute-done((bf16[16,96,128]{2,1,0:T(8,128)(2,1)S(1)}, bf16[16,96,128]{2,1,0:T(8,128)(2,1)S(1)}, u32[]{:S(2)}, u32[]{:S(2)}) %collective-permute-start.1) | collective-permute-done | bytes 393248 | tf_op jit(solution)/shard_map/ppermute | solution.py:189
  48.9 0.8 %shard_map.43.refs_1_ = f32[2,512,256]{2,1,0:T(8,128)S(1)} custom-call(bf16[16,96,128]{2,1,0:T(8,128)(2,1)S(1)} %collective-permute-done.1.block_ref, f32[2,512,256]{2,1,0:T(8,128)S(1)} %shard_map.42.in_ref, bf16[512,4096]{1,0:T(8,128)(2,1)S(1)} %shard_map.40.own_ref.refs_2_, bf16[512,4096]{1,0:T(8,128)(2,1)S(1)} %shard_map.41.other_ref.refs_3_), custom_call_target="tpu_custom_call" | custom-call | flops 402653184 | bytes 3145728 | tf_op jit(solution)/shard_map/pallas_call | solution.py:151
  49.8 0.0 collective-permute-done.refs_0_
  49.8 1.0 %shard_map.44 = f32[384,512]{1,0:T(8,128)S(1)} custom-call(bf16[16,96,128]{2,1,0:T(8,128)(2,1)S(1)} %collective-permute-done.refs_0_, f32[2,512,256]{2,1,0:T(8,128)S(1)} %shard_map.43.refs_1_, bf16[512,4096]{1,0:T(8,128)(2,1)S(1)} %shard_map.40.own_ref.refs_2_, bf16[512,4096]{1,0:T(8,128)(2,1)S(1)} %shard_map.41.other_ref.refs_3_), custom_call_target="tpu_custom_call" | custom-call | flops 402653184 | bytes 3145728 | tf_op jit(solution)/shard_map/pallas_call | solution.py:166
  50.8 0.1 convert_element_type.15
  50.9 19.8 %all_to_all.18 = f16[16,24,512]{2,1,0:T(8,128)(2,1)S(1)} all-to-all(f16[16,24,512]{2,1,0:T(8,128)(2,1)S(1)} %bitcast.8), channel_id=1, replica_groups=mesh['z'=8,'x'=4,'c'=2,'y'=8] {'c','y'}, dimensions={0} | all-to-all | bytes 786432 | tf_op jit(solution)/shard_map/all_to_all | solution.py:195
  70.7 0.1 convert_reduce_fusion
  70.8 0.6 multiply_convert_fusion
Async XLA Ops:
  0.0 0.8 %copy-start.1 = (bf16[384,64]{0,1:T(8,128)(2,1)S(1)}, bf16[384,64]{0,1:T(8,128)(2,1)}, u32[]{:S(2)}) copy-start(bf16[384,64]{0,1:T(8,128)(2,1)} %param.3) | copy-start | bytes 147460
  1.8 24.3 %all-to-all-start = ((bf16[16,96,128]{2,1,0:T(8,128)(2,1)}), bf16[16,96,128]{2,1,0:T(8,128)(2,1)S(1)}, u32[]{:S(2)}, u32[]{:S(2)}) async-start(bf16[16,96,128]{2,1,0:T(8,128)(2,1)} %bitcast.1), calls=%async_computation | async-start | bytes 786432 | tf_op jit(solution)/shard_map/all_to_all | solution.py:185
  13.7 2.2 %copy-start = (bf16[512,4096]{1,0:T(8,128)(2,1)S(1)}, bf16[512,4096]{1,0:T(8,128)(2,1)}, u32[]{:S(2)}) copy-start(bf16[512,4096]{1,0:T(8,128)(2,1)} %m_ref.1) | copy-start | bytes 12582916
  15.8 0.7 copy-start.2
  20.2 22.0 %collective-permute-start.3 = (bf16[512,4096]{1,0:T(8,128)(2,1)}, bf16[512,4096]{1,0:T(8,128)(2,1)}, u32[]{:S(2)}, u32[]{:S(2)}) collective-permute-start(bf16[512,4096]{1,0:T(8,128)(2,1)} %shard_map.38.own_ref.m_ref), channel_id=1, source_target_pairs={{0,8},{8,0},{1,9},{9,1},{2,10},{10,2},{3,11},{11,3},{4,12},{12,4},... | collective-permute-start | bytes 12582920 | tf_op jit(solution)/shard_map/ppermute | solution.py:187
  26.1 18.3 %collective-permute-start.2 = (bf16[16,96,128]{2,1,0:T(8,128)(2,1)S(1)}, bf16[16,96,128]{2,1,0:T(8,128)(2,1)S(1)}, u32[]{:S(2)}, u32[]{:S(2)}) collective-permute-start(bf16[16,96,128]{2,1,0:T(8,128)(2,1)S(1)} %all-to-all-done.block_ref), channel_id=1, source_target_pairs={{0,32},{16,48},{32,0},{48,16},{1,33},{17,49},{33,1},{49,17},{2,34}... | collective-permute-start | bytes 1179656 | tf_op jit(solution)/shard_map/ppermute | solution.py:189
  30.7 18.2 %collective-permute-start.1 = (bf16[16,96,128]{2,1,0:T(8,128)(2,1)S(1)}, bf16[16,96,128]{2,1,0:T(8,128)(2,1)S(1)}, u32[]{:S(2)}, u32[]{:S(2)}) collective-permute-start(bf16[16,96,128]{2,1,0:T(8,128)(2,1)S(1)} %all-to-all-done.block_ref), channel_id=1, source_target_pairs={{0,16},{16,32},{32,48},{48,0},{1,17},{17,33},{33,49},{49,1},{2,18}... | collective-permute-start | bytes 1179656 | tf_op jit(solution)/shard_map/ppermute | solution.py:189
  33.0 16.8 %collective-permute-start = (bf16[16,96,128]{2,1,0:T(8,128)(2,1)S(1)}, bf16[16,96,128]{2,1,0:T(8,128)(2,1)S(1)}, u32[]{:S(2)}, u32[]{:S(2)}) collective-permute-start(bf16[16,96,128]{2,1,0:T(8,128)(2,1)S(1)} %all-to-all-done.block_ref), channel_id=1, source_target_pairs={{0,48},{16,0},{32,16},{48,32},{1,49},{17,1},{33,17},{49,33},{2,50}... | collective-permute-start | bytes 1179656 | tf_op jit(solution)/shard_map/ppermute | solution.py:189

commit v8 on v7

--- a/solution.py
+++ b/solution.py
@@ -122,18 +122,13 @@
     acc_ref[1] += block_dot(other_ref, w, source(2))
 
 
-def next_kernel(block_ref, in_ref, own_ref, other_ref, acc_ref, w_ref):
-    spread(block_ref, w_ref)
-    w = w_ref[...]
-    for i, m_ref in enumerate((own_ref, other_ref)):
-        acc_ref[i] = in_ref[i] + block_dot(m_ref, w, source(1))
-
-
-def last_kernel(shift, block_ref, in_ref, own_ref, other_ref, out_ref, w_ref, acc_ref):
-    spread(block_ref, w_ref)
-    w = w_ref[...]
-    for i, m_ref in enumerate((own_ref, other_ref)):
-        acc_ref[i] = in_ref[i] + block_dot(m_ref, w, source(shift))
+def last_kernel(shifts, first_ref, second_ref, in_ref, own_ref, other_ref, out_ref, w_ref, acc_ref):
+    for n, block_ref in enumerate((first_ref, second_ref)):
+        spread(block_ref, w_ref)
+        w = w_ref[...]
+        for i, m_ref in enumerate((own_ref, other_ref)):
+            before = in_ref[i] if n == 0 else acc_ref[i]
+            acc_ref[i] = before + block_dot(m_ref, w, source(shifts[n]))
     own, other = [(acc_ref[i] * SCALE).T[:HALF] for i in range(NC)]
     leads = lax.axis_index("c") == 0
     sums = jnp.where(leads, own, other), jnp.where(leads, other, own)
@@ -159,19 +154,19 @@
     )(*args)
 
 
-def last_dots(shift, block, acc, own, other):
+def last_dots(shifts, blocks, acc, own, other):
     def last(*refs):
-        last_kernel(shift, *refs)
+        last_kernel(shifts, *refs)
 
     return pl.pallas_call(
         last,
-        in_specs=[pl.BlockSpec(memory_space=pltpu.VMEM)] * 4,
+        in_specs=[pl.BlockSpec(memory_space=pltpu.VMEM)] * 5,
         out_specs=pl.BlockSpec(memory_space=pltpu.VMEM),
         out_shape=jax.ShapeDtypeStruct((OP, ROWS), jnp.float32),
         scratch_shapes=[pltpu.VMEM((WIDE, 256), jnp.bfloat16), pltpu.VMEM(ACC, jnp.float32)],
         compiler_params=pltpu.CompilerParams(vmem_limit_bytes=16 << 20),
-        cost_estimate=pl.CostEstimate(flops=OP * ROWS * COLS // 2, bytes_accessed=3 << 20, transcendentals=0),
-    )(block, acc, own, other)
+        cost_estimate=pl.CostEstimate(flops=OP * ROWS * COLS, bytes_accessed=3 << 20, transcendentals=0),
+    )(*blocks, acc, own, other)
 
 
 SHIFTS = (2, 1, 3)
@@ -190,8 +185,7 @@
     acc = some_dots(own_kernel, ACC[1:], HIDE, block, own)
     own, other = load(own, acc), load(other, acc)
     acc = some_dots(two_kernel, ACC, OP * ROWS * COLS, block, far, acc, own, other)
-    acc = some_dots(next_kernel, ACC, OP * ROWS * COLS // 2, right, acc, own, other)
-    partial_sums = last_dots(3, left, acc, own, other).astype(jnp.float16)
+    partial_sums = last_dots((1, 3), (right, left), acc, own, other).astype(jnp.float16)
     landed = lax.all_to_all(partial_sums, ("c", "y"), 0, 0, tiled=True)
     total = jnp.sum(landed.reshape(NC, NY, SEG, ROWS).astype(jnp.float32), axis=1).reshape(NC * SEG, ROWS)
     return (total * (1.0 / SCALE)).astype(jnp.bfloat16)

time: 72.2 us -> 72 us (level)
    pallas_call x3 -> x2, Pallas kernels: 4.68 us -> 3.86 us  [some_dots(): pl.pallas_call(kernel, in_specs=[pl.BlockSpec(memory_space=pltpu.VMEM)] *...]
  transfers between devices with their start and end apart: 5 -> 5, of which waited for: 2 -> 2; matrix products, arithmetic and copies ran while one was open for 0% -> 0% of each run, Pallas kernels for 18% -> 17%
where the time goes in v8:
time: 72 us; the launch traced here: 71.3 us
  starting transfers between devices  25 us (35%)
  blocking collectives  19.9 us (28%)
  Pallas kernels  14.6 us (20%)
  waiting for transfers between devices  7.26 us (10%)
  local copies, waits for them, and re-layouts  3.66 us (5%)
  other arithmetic  0.74 us (1%)
    all_to_all x1, blocking collectives, shards(): landed = lax.all_to_all(partial_sums, ('c', 'y'), 0, 0, tiled=True)  19.9 us
    all_to_all x1, starting transfers between devices, shards(): lax.all_to_all(pieces.reshape(NZ * NC * 96, 128), ('c', 'z'), 0, 0, tiled...  11.8 us
    ppermute x3, starting transfers between devices, shards(): lax.ppermute(block, 'x', [(i, (i + d) % NX) for i in range(NX)])  11.1 us
    pallas_call x2, Pallas kernels, load(): pl.pallas_call(load_kernel, in_specs=[pl.BlockSpec(memory_space=pl.ANY)]...  4.4 us
    all_to_all x1, waiting for transfers between devices, shards(): lax.all_to_all(pieces.reshape(NZ * NC * 96, 128), ('c', 'z'), 0, 0, tiled...  3.87 us
    pallas_call x2, Pallas kernels, some_dots(): pl.pallas_call(kernel, in_specs=[pl.BlockSpec(memory_space=pltpu.VMEM)] *...  3.86 us
    pallas_call x1, Pallas kernels, mask(): pl.pallas_call(mask_kernel, in_specs=[pl.BlockSpec(memory_space=pltpu.SME...  3.7 us
    unnamed x6, local copies, waits for them, and re-layouts  3.66 us
  transfers between devices with their start and end apart: 5, of which 2 were waited for; matrix products, arithmetic and copies ran while one was open for 0% of the time, Pallas kernels for 17%

profile of v8, /device:TPU:1, one launch (start us, length us, event | category | flops | bytes accessed | tf_op | source)
XLA Modules:
  0.0 71.3 jit_solution(16228756342136438995)
XLA Ops:
  0.0 0.0 copy-start.1
  0.0 0.8 %copy-done.1 = bf16[384,64]{0,1:T(8,128)(2,1)S(1)} copy-done((bf16[384,64]{0,1:T(8,128)(2,1)S(1)}, bf16[384,64]{0,1:T(8,128)(2,1)}, u32[]{:S(2)}) %copy-start.1) | copy-done | bytes 49176
  0.8 1.0 %shard_map.37 = bf16[2,8,96,128]{3,2,1,0:T(8,128)(2,1)} custom-call(bf16[64,384]{1,0:T(8,128)(2,1)S(1)} %bitcast.7), custom_call_target="tpu_custom_call" | custom-call | flops 25165824 | bytes 450000 | tf_op jit(solution)/shard_map/pallas_call | solution.py:41
  1.8 11.8 %all-to-all-start = ((bf16[16,96,128]{2,1,0:T(8,128)(2,1)}), bf16[16,96,128]{2,1,0:T(8,128)(2,1)S(1)}, u32[]{:S(2)}, u32[]{:S(2)}) async-start(bf16[16,96,128]{2,1,0:T(8,128)(2,1)} %bitcast.1), calls=%async_computation | async-start | bytes 786432 | tf_op jit(solution)/shard_map/all_to_all | solution.py:180
  13.7 0.0 copy-start
  13.7 2.2 %copy-done = bf16[512,4096]{1,0:T(8,128)(2,1)S(1)} copy-done((bf16[512,4096]{1,0:T(8,128)(2,1)S(1)}, bf16[512,4096]{1,0:T(8,128)(2,1)}, u32[]{:S(2)}) %copy-start) | copy-done | bytes 4194328
  15.8 0.0 copy-start.2
  15.8 0.7 copy-done.2
  16.5 3.7 %shard_map.38.own_ref.m_ref = bf16[512,4096]{1,0:T(8,128)(2,1)} custom-call(s32[4,32]{1,0:T(4,128)S(1)} %copy-done.2, bf16[512,4096]{1,0:T(8,128)(2,1)S(1)} %copy-done), custom_call_target="tpu_custom_call" | custom-call | flops 2097152 | bytes 8388608 | tf_op jit(solution)/shard_map/pallas_call | solution.py:63
  20.2 2.0 %collective-permute-start.3 = (bf16[512,4096]{1,0:T(8,128)(2,1)}, bf16[512,4096]{1,0:T(8,128)(2,1)}, u32[]{:S(2)}, u32[]{:S(2)}) collective-permute-start(bf16[512,4096]{1,0:T(8,128)(2,1)} %shard_map.38.own_ref.m_ref), channel_id=1, source_target_pairs={{0,8},{8,0},{1,9},{9,1},{2,10},{10,2},{3,11},{11,3},{4,12},{12,4},... | collective-permute-start | bytes 12582920 | tf_op jit(solution)/shard_map/ppermute | solution.py:182
  22.2 3.9 %all-to-all-done.block_ref = bf16[16,96,128]{2,1,0:T(8,128)(2,1)S(1)} async-done(((bf16[16,96,128]{2,1,0:T(8,128)(2,1)}), bf16[16,96,128]{2,1,0:T(8,128)(2,1)S(1)}, u32[]{:S(2)}, u32[]{:S(2)}) %all-to-all-start) | async-done | bytes 393248 | tf_op jit(solution)/shard_map/all_to_all | solution.py:180
  26.1 4.6 %collective-permute-start.2 = (bf16[16,96,128]{2,1,0:T(8,128)(2,1)S(1)}, bf16[16,96,128]{2,1,0:T(8,128)(2,1)S(1)}, u32[]{:S(2)}, u32[]{:S(2)}) collective-permute-start(bf16[16,96,128]{2,1,0:T(8,128)(2,1)S(1)} %all-to-all-done.block_ref), channel_id=1, source_target_pairs={{0,32},{16,48},{32,0},{48,16},{1,33},{17,49},{33,1},{49,17},{2,34}... | collective-permute-start | bytes 1179656 | tf_op jit(solution)/shard_map/ppermute | solution.py:184
  30.7 2.2 %collective-permute-start = (bf16[16,96,128]{2,1,0:T(8,128)(2,1)S(1)}, bf16[16,96,128]{2,1,0:T(8,128)(2,1)S(1)}, u32[]{:S(2)}, u32[]{:S(2)}) collective-permute-start(bf16[16,96,128]{2,1,0:T(8,128)(2,1)S(1)} %all-to-all-done.block_ref), channel_id=1, source_target_pairs={{0,16},{16,32},{32,48},{48,0},{1,17},{17,33},{33,49},{49,1},{2,18}... | collective-permute-start | bytes 1179656 | tf_op jit(solution)/shard_map/ppermute | solution.py:184
  33.0 4.3 %collective-permute-start.1 = (bf16[16,96,128]{2,1,0:T(8,128)(2,1)S(1)}, bf16[16,96,128]{2,1,0:T(8,128)(2,1)S(1)}, u32[]{:S(2)}, u32[]{:S(2)}) collective-permute-start(bf16[16,96,128]{2,1,0:T(8,128)(2,1)S(1)} %all-to-all-done.block_ref), channel_id=1, source_target_pairs={{0,48},{16,0},{32,16},{48,32},{1,49},{17,1},{33,17},{49,33},{2,50}... | collective-permute-start | bytes 1179656 | tf_op jit(solution)/shard_map/ppermute | solution.py:184
  37.2 2.7 %shard_map.39.after_ref.acc_own_ref = f32[512,256]{1,0:T(8,128)S(1)} custom-call(bf16[16,96,128]{2,1,0:T(8,128)(2,1)S(1)} %all-to-all-done.block_ref, bf16[512,4096]{1,0:T(8,128)(2,1)} %shard_map.38.own_ref.m_ref), custom_call_target="tpu_custom_call" | custom-call | flops 68719476736 | bytes 3145728 | tf_op jit(solution)/shard_map/pallas_call | solution.py:146
  40.0 2.2 %shard_map.40.own_ref.refs_3_ = bf16[512,4096]{1,0:T(8,128)(2,1)S(1)} custom-call(bf16[512,4096]{1,0:T(8,128)(2,1)} %shard_map.38.own_ref.m_ref, f32[512,256]{1,0:T(8,128)S(1)} %shard_map.39.after_ref.acc_own_ref), custom_call_target="tpu_custom_call" | custom-call | bytes 8388608 | tf_op jit(solution)/shard_map/pallas_call | solution.py:100
  42.2 0.0 collective-permute-done.3.m_ref
  42.2 2.2 %shard_map.41.other_ref.refs_4_ = bf16[512,4096]{1,0:T(8,128)(2,1)S(1)} custom-call(bf16[512,4096]{1,0:T(8,128)(2,1)} %collective-permute-done.3.m_ref, f32[512,256]{1,0:T(8,128)S(1)} %shard_map.39.after_ref.acc_own_ref), custom_call_target="tpu_custom_call" | custom-call | bytes 8388608 | tf_op jit(solution)/shard_map/pallas_call | solution.py:100
  44.4 0.0 collective-permute-done.2.far_ref
  44.4 1.1 %shard_map.42.refs_2_ = f32[2,512,256]{2,1,0:T(8,128)S(1)} custom-call(bf16[16,96,128]{2,1,0:T(8,128)(2,1)S(1)} %all-to-all-done.block_ref, bf16[16,96,128]{2,1,0:T(8,128)(2,1)S(1)} %collective-permute-done.2.far_ref, f32[512,256]{1,0:T(8,128)S(1)} %shard_map.39.after_ref.acc_own_ref, bf16[512,4096]{1,0:T(8,128)(2,1)S(1)} %shard_map.40.own_ref.refs_3_, ...), custom_call_target="tpu_custom_call" | custom-call | flops 805306368 | bytes 3145728 | tf_op jit(solution)/shard_map/pallas_call | solution.py:146
  45.6 3.4 %collective-permute-done.refs_0_ = bf16[16,96,128]{2,1,0:T(8,128)(2,1)S(1)} collective-permute-done((bf16[16,96,128]{2,1,0:T(8,128)(2,1)S(1)}, bf16[16,96,128]{2,1,0:T(8,128)(2,1)S(1)}, u32[]{:S(2)}, u32[]{:S(2)}) %collective-permute-start) | collective-permute-done | bytes 393248 | tf_op jit(solution)/shard_map/ppermute | solution.py:184
  48.9 0.0 collective-permute-done.1.refs_1_
  48.9 1.7 %shard_map.43 = f32[384,512]{1,0:T(8,128)S(1)} custom-call(bf16[16,96,128]{2,1,0:T(8,128)(2,1)S(1)} %collective-permute-done.refs_0_, bf16[16,96,128]{2,1,0:T(8,128)(2,1)S(1)} %collective-permute-done.1.refs_1_, f32[2,512,256]{2,1,0:T(8,128)S(1)} %shard_map.42.refs_2_, bf16[512,4096]{1,0:T(8,128)(2,1)S(1)} %shard_map.40.own_ref.refs_3_, ...), custom_call_target="tpu_custom_call" | custom-call | flops 805306368 | bytes 3145728 | tf_op jit(solution)/shard_map/pallas_call | solution.py:161
  50.6 0.1 convert_element_type.15
  50.7 19.9 %all_to_all.18 = f16[16,24,512]{2,1,0:T(8,128)(2,1)S(1)} all-to-all(f16[16,24,512]{2,1,0:T(8,128)(2,1)S(1)} %bitcast.8), channel_id=1, replica_groups=mesh['z'=8,'x'=4,'c'=2,'y'=8] {'c','y'}, dimensions={0} | all-to-all | bytes 786432 | tf_op jit(solution)/shard_map/all_to_all | solution.py:189
  70.6 0.1 convert_reduce_fusion
  70.7 0.6 multiply_convert_fusion
Async XLA Ops:
  0.0 0.8 %copy-start.1 = (bf16[384,64]{0,1:T(8,128)(2,1)S(1)}, bf16[384,64]{0,1:T(8,128)(2,1)}, u32[]{:S(2)}) copy-start(bf16[384,64]{0,1:T(8,128)(2,1)} %param.3) | copy-start | bytes 147460
  1.8 24.3 %all-to-all-start = ((bf16[16,96,128]{2,1,0:T(8,128)(2,1)}), bf16[16,96,128]{2,1,0:T(8,128)(2,1)S(1)}, u32[]{:S(2)}, u32[]{:S(2)}) async-start(bf16[16,96,128]{2,1,0:T(8,128)(2,1)} %bitcast.1), calls=%async_computation | async-start | bytes 786432 | tf_op jit(solution)/shard_map/all_to_all | solution.py:180
  13.7 2.2 %copy-start = (bf16[512,4096]{1,0:T(8,128)(2,1)S(1)}, bf16[512,4096]{1,0:T(8,128)(2,1)}, u32[]{:S(2)}) copy-start(bf16[512,4096]{1,0:T(8,128)(2,1)} %m_ref.1) | copy-start | bytes 12582916
  15.8 0.7 copy-start.2
  20.2 22.0 %collective-permute-start.3 = (bf16[512,4096]{1,0:T(8,128)(2,1)}, bf16[512,4096]{1,0:T(8,128)(2,1)}, u32[]{:S(2)}, u32[]{:S(2)}) collective-permute-start(bf16[512,4096]{1,0:T(8,128)(2,1)} %shard_map.38.own_ref.m_ref), channel_id=1, source_target_pairs={{0,8},{8,0},{1,9},{9,1},{2,10},{10,2},{3,11},{11,3},{4,12},{12,4},... | collective-permute-start | bytes 12582920 | tf_op jit(solution)/shard_map/ppermute | solution.py:182
  26.1 18.3 %collective-permute-start.2 = (bf16[16,96,128]{2,1,0:T(8,128)(2,1)S(1)}, bf16[16,96,128]{2,1,0:T(8,128)(2,1)S(1)}, u32[]{:S(2)}, u32[]{:S(2)}) collective-permute-start(bf16[16,96,128]{2,1,0:T(8,128)(2,1)S(1)} %all-to-all-done.block_ref), channel_id=1, source_target_pairs={{0,32},{16,48},{32,0},{48,16},{1,33},{17,49},{33,1},{49,17},{2,34}... | collective-permute-start | bytes 1179656 | tf_op jit(solution)/shard_map/ppermute | solution.py:184
  30.7 18.2 %collective-permute-start = (bf16[16,96,128]{2,1,0:T(8,128)(2,1)S(1)}, bf16[16,96,128]{2,1,0:T(8,128)(2,1)S(1)}, u32[]{:S(2)}, u32[]{:S(2)}) collective-permute-start(bf16[16,96,128]{2,1,0:T(8,128)(2,1)S(1)} %all-to-all-done.block_ref), channel_id=1, source_target_pairs={{0,16},{16,32},{32,48},{48,0},{1,17},{17,33},{33,49},{49,1},{2,18}... | collective-permute-start | bytes 1179656 | tf_op jit(solution)/shard_map/ppermute | solution.py:184
  33.0 16.0 %collective-permute-start.1 = (bf16[16,96,128]{2,1,0:T(8,128)(2,1)S(1)}, bf16[16,96,128]{2,1,0:T(8,128)(2,1)S(1)}, u32[]{:S(2)}, u32[]{:S(2)}) collective-permute-start(bf16[16,96,128]{2,1,0:T(8,128)(2,1)S(1)} %all-to-all-done.block_ref), channel_id=1, source_target_pairs={{0,48},{16,0},{32,16},{48,32},{1,49},{17,1},{33,17},{49,33},{2,50}... | collective-permute-start | bytes 1179656 | tf_op jit(solution)/shard_map/ppermute | solution.py:184

commit v9 on v7

--- a/solution.py
+++ b/solution.py
@@ -193,8 +193,8 @@
     acc = some_dots(next_kernel, ACC, OP * ROWS * COLS // 2, right, acc, own, other)
     partial_sums = last_dots(3, left, acc, own, other).astype(jnp.float16)
     landed = lax.all_to_all(partial_sums, ("c", "y"), 0, 0, tiled=True)
-    total = jnp.sum(landed.reshape(NC, NY, SEG, ROWS).astype(jnp.float32), axis=1).reshape(NC * SEG, ROWS)
-    return (total * (1.0 / SCALE)).astype(jnp.bfloat16)
+    parts = landed.reshape(NC, NY, SEG, ROWS).astype(jnp.float32) * (1.0 / SCALE)
+    return jnp.sum(parts, axis=1).reshape(NC * SEG, ROWS).astype(jnp.bfloat16)
 
 
 def solution(mesh):

time: 72.2 us -> 72.2 us (level)
  no operation moved by 1% of the time
where the time goes in v9:
time: 72.2 us; the launch traced here: 71.4 us
  starting transfers between devices  25 us (35%)
  blocking collectives  19.8 us (27%)
  Pallas kernels  14.8 us (20%)
  waiting for transfers between devices  7.26 us (10%)
  local copies, waits for them, and re-layouts  3.66 us (5%)
  other arithmetic  0.75 us (1%)
    all_to_all x1, blocking collectives, shards(): landed = lax.all_to_all(partial_sums, ('c', 'y'), 0, 0, tiled=True)  19.8 us
    all_to_all x1, starting transfers between devices, shards(): lax.all_to_all(pieces.reshape(NZ * NC * 96, 128), ('c', 'z'), 0, 0, tiled...  11.8 us
    ppermute x3, starting transfers between devices, shards(): lax.ppermute(block, 'x', [(i, (i + d) % NX) for i in range(NX)])  11.1 us
    pallas_call x3, Pallas kernels, some_dots(): pl.pallas_call(kernel, in_specs=[pl.BlockSpec(memory_space=pltpu.VMEM)] *...  4.68 us
    pallas_call x2, Pallas kernels, load(): pl.pallas_call(load_kernel, in_specs=[pl.BlockSpec(memory_space=pl.ANY)]...  4.4 us
    all_to_all x1, waiting for transfers between devices, shards(): lax.all_to_all(pieces.reshape(NZ * NC * 96, 128), ('c', 'z'), 0, 0, tiled...  3.87 us
    pallas_call x1, Pallas kernels, mask(): pl.pallas_call(mask_kernel, in_specs=[pl.BlockSpec(memory_space=pltpu.SME...  3.7 us
    unnamed x6, local copies, waits for them, and re-layouts  3.66 us
  transfers between devices with their start and end apart: 5, of which 2 were waited for; matrix products, arithmetic and copies ran while one was open for 0% of the time, Pallas kernels for 18%

profile of v9, /device:TPU:1, one launch (start us, length us, event | category | flops | bytes accessed | tf_op | source)
XLA Modules:
  0.0 71.4 jit_solution(17979277275753086327)
XLA Ops:
  0.0 0.0 copy-start.1
  0.0 0.8 %copy-done.1 = bf16[384,64]{0,1:T(8,128)(2,1)S(1)} copy-done((bf16[384,64]{0,1:T(8,128)(2,1)S(1)}, bf16[384,64]{0,1:T(8,128)(2,1)}, u32[]{:S(2)}) %copy-start.1) | copy-done | bytes 49176
  0.8 1.0 %shard_map.37 = bf16[2,8,96,128]{3,2,1,0:T(8,128)(2,1)} custom-call(bf16[64,384]{1,0:T(8,128)(2,1)S(1)} %bitcast.6), custom_call_target="tpu_custom_call" | custom-call | flops 25165824 | bytes 450000 | tf_op jit(solution)/shard_map/pallas_call | solution.py:41
  1.8 11.8 %all-to-all-start = ((bf16[16,96,128]{2,1,0:T(8,128)(2,1)}), bf16[16,96,128]{2,1,0:T(8,128)(2,1)S(1)}, u32[]{:S(2)}, u32[]{:S(2)}) async-start(bf16[16,96,128]{2,1,0:T(8,128)(2,1)} %bitcast.1), calls=%async_computation | async-start | bytes 786432 | tf_op jit(solution)/shard_map/all_to_all | solution.py:185
  13.7 0.0 copy-start
  13.7 2.2 %copy-done = bf16[512,4096]{1,0:T(8,128)(2,1)S(1)} copy-done((bf16[512,4096]{1,0:T(8,128)(2,1)S(1)}, bf16[512,4096]{1,0:T(8,128)(2,1)}, u32[]{:S(2)}) %copy-start) | copy-done | bytes 4194328
  15.8 0.0 copy-start.2
  15.8 0.7 copy-done.2
  16.5 3.7 %shard_map.38.own_ref.m_ref = bf16[512,4096]{1,0:T(8,128)(2,1)} custom-call(s32[4,32]{1,0:T(4,128)S(1)} %copy-done.2, bf16[512,4096]{1,0:T(8,128)(2,1)S(1)} %copy-done), custom_call_target="tpu_custom_call" | custom-call | flops 2097152 | bytes 8388608 | tf_op jit(solution)/shard_map/pallas_call | solution.py:63
  20.2 2.0 %collective-permute-start.3 = (bf16[512,4096]{1,0:T(8,128)(2,1)}, bf16[512,4096]{1,0:T(8,128)(2,1)}, u32[]{:S(2)}, u32[]{:S(2)}) collective-permute-start(bf16[512,4096]{1,0:T(8,128)(2,1)} %shard_map.38.own_ref.m_ref), channel_id=1, source_target_pairs={{0,8},{8,0},{1,9},{9,1},{2,10},{10,2},{3,11},{11,3},{4,12},{12,4},... | collective-permute-start | bytes 12582920 | tf_op jit(solution)/shard_map/ppermute | solution.py:187
  22.2 3.9 %all-to-all-done.block_ref = bf16[16,96,128]{2,1,0:T(8,128)(2,1)S(1)} async-done(((bf16[16,96,128]{2,1,0:T(8,128)(2,1)}), bf16[16,96,128]{2,1,0:T(8,128)(2,1)S(1)}, u32[]{:S(2)}, u32[]{:S(2)}) %all-to-all-start) | async-done | bytes 393248 | tf_op jit(solution)/shard_map/all_to_all | solution.py:185
  26.1 4.6 %collective-permute-start.2 = (bf16[16,96,128]{2,1,0:T(8,128)(2,1)S(1)}, bf16[16,96,128]{2,1,0:T(8,128)(2,1)S(1)}, u32[]{:S(2)}, u32[]{:S(2)}) collective-permute-start(bf16[16,96,128]{2,1,0:T(8,128)(2,1)S(1)} %all-to-all-done.block_ref), channel_id=1, source_target_pairs={{0,32},{16,48},{32,0},{48,16},{1,33},{17,49},{33,1},{49,17},{2,34}... | collective-permute-start | bytes 1179656 | tf_op jit(solution)/shard_map/ppermute | solution.py:189
  30.7 2.2 %collective-permute-start.1 = (bf16[16,96,128]{2,1,0:T(8,128)(2,1)S(1)}, bf16[16,96,128]{2,1,0:T(8,128)(2,1)S(1)}, u32[]{:S(2)}, u32[]{:S(2)}) collective-permute-start(bf16[16,96,128]{2,1,0:T(8,128)(2,1)S(1)} %all-to-all-done.block_ref), channel_id=1, source_target_pairs={{0,16},{16,32},{32,48},{48,0},{1,17},{17,33},{33,49},{49,1},{2,18}... | collective-permute-start | bytes 1179656 | tf_op jit(solution)/shard_map/ppermute | solution.py:189
  33.0 4.3 %collective-permute-start = (bf16[16,96,128]{2,1,0:T(8,128)(2,1)S(1)}, bf16[16,96,128]{2,1,0:T(8,128)(2,1)S(1)}, u32[]{:S(2)}, u32[]{:S(2)}) collective-permute-start(bf16[16,96,128]{2,1,0:T(8,128)(2,1)S(1)} %all-to-all-done.block_ref), channel_id=1, source_target_pairs={{0,48},{16,0},{32,16},{48,32},{1,49},{17,1},{33,17},{49,33},{2,50}... | collective-permute-start | bytes 1179656 | tf_op jit(solution)/shard_map/ppermute | solution.py:189
  37.2 2.7 %shard_map.39.after_ref.acc_own_ref = f32[512,256]{1,0:T(8,128)S(1)} custom-call(bf16[16,96,128]{2,1,0:T(8,128)(2,1)S(1)} %all-to-all-done.block_ref, bf16[512,4096]{1,0:T(8,128)(2,1)} %shard_map.38.own_ref.m_ref), custom_call_target="tpu_custom_call" | custom-call | flops 68719476736 | bytes 3145728 | tf_op jit(solution)/shard_map/pallas_call | solution.py:151
  40.0 2.2 %shard_map.40.own_ref.refs_2_ = bf16[512,4096]{1,0:T(8,128)(2,1)S(1)} custom-call(bf16[512,4096]{1,0:T(8,128)(2,1)} %shard_map.38.own_ref.m_ref, f32[512,256]{1,0:T(8,128)S(1)} %shard_map.39.after_ref.acc_own_ref), custom_call_target="tpu_custom_call" | custom-call | bytes 8388608 | tf_op jit(solution)/shard_map/pallas_call | solution.py:100
  42.2 0.0 collective-permute-done.3.m_ref
  42.2 2.2 %shard_map.41.other_ref.refs_3_ = bf16[512,4096]{1,0:T(8,128)(2,1)S(1)} custom-call(bf16[512,4096]{1,0:T(8,128)(2,1)} %collective-permute-done.3.m_ref, f32[512,256]{1,0:T(8,128)S(1)} %shard_map.39.after_ref.acc_own_ref), custom_call_target="tpu_custom_call" | custom-call | bytes 8388608 | tf_op jit(solution)/shard_map/pallas_call | solution.py:100
  44.4 0.0 collective-permute-done.2.far_ref
  44.4 1.1 %shard_map.42.in_ref = f32[2,512,256]{2,1,0:T(8,128)S(1)} custom-call(bf16[16,96,128]{2,1,0:T(8,128)(2,1)S(1)} %all-to-all-done.block_ref, bf16[16,96,128]{2,1,0:T(8,128)(2,1)S(1)} %collective-permute-done.2.far_ref, f32[512,256]{1,0:T(8,128)S(1)} %shard_map.39.after_ref.acc_own_ref, bf16[512,4096]{1,0:T(8,128)(2,1)S(1)} %shard_map.40.own_ref.refs_2_, ...), custom_call_target="tpu_custom_call" | custom-call | flops 805306368 | bytes 3145728 | tf_op jit(solution)/shard_map/pallas_call | solution.py:151
  45.6 3.4 %collective-permute-done.1.block_ref = bf16[16,96,128]{2,1,0:T(8,128)(2,1)S(1)} collective-permute-done((bf16[16,96,128]{2,1,0:T(8,128)(2,1)S(1)}, bf16[16,96,128]{2,1,0:T(8,128)(2,1)S(1)}, u32[]{:S(2)}, u32[]{:S(2)}) %collective-permute-start.1) | collective-permute-done | bytes 393248 | tf_op jit(solution)/shard_map/ppermute | solution.py:189
  48.9 0.8 %shard_map.43.refs_1_ = f32[2,512,256]{2,1,0:T(8,128)S(1)} custom-call(bf16[16,96,128]{2,1,0:T(8,128)(2,1)S(1)} %collective-permute-done.1.block_ref, f32[2,512,256]{2,1,0:T(8,128)S(1)} %shard_map.42.in_ref, bf16[512,4096]{1,0:T(8,128)(2,1)S(1)} %shard_map.40.own_ref.refs_2_, bf16[512,4096]{1,0:T(8,128)(2,1)S(1)} %shard_map.41.other_ref.refs_3_), custom_call_target="tpu_custom_call" | custom-call | flops 402653184 | bytes 3145728 | tf_op jit(solution)/shard_map/pallas_call | solution.py:151
  49.8 0.0 collective-permute-done.refs_0_
  49.8 1.0 %shard_map.44 = f32[384,512]{1,0:T(8,128)S(1)} custom-call(bf16[16,96,128]{2,1,0:T(8,128)(2,1)S(1)} %collective-permute-done.refs_0_, f32[2,512,256]{2,1,0:T(8,128)S(1)} %shard_map.43.refs_1_, bf16[512,4096]{1,0:T(8,128)(2,1)S(1)} %shard_map.40.own_ref.refs_2_, bf16[512,4096]{1,0:T(8,128)(2,1)S(1)} %shard_map.41.other_ref.refs_3_), custom_call_target="tpu_custom_call" | custom-call | flops 402653184 | bytes 3145728 | tf_op jit(solution)/shard_map/pallas_call | solution.py:166
  50.8 0.1 convert_element_type.13
  50.9 19.8 %all_to_all.18 = f16[16,24,512]{2,1,0:T(8,128)(2,1)S(1)} all-to-all(f16[16,24,512]{2,1,0:T(8,128)(2,1)S(1)} %bitcast.7), channel_id=1, replica_groups=mesh['z'=8,'x'=4,'c'=2,'y'=8] {'c','y'}, dimensions={0} | all-to-all | bytes 786432 | tf_op jit(solution)/shard_map/all_to_all | solution.py:195
  70.7 0.7 bitcast_reduce_fusion
Async XLA Ops:
  0.0 0.8 %copy-start.1 = (bf16[384,64]{0,1:T(8,128)(2,1)S(1)}, bf16[384,64]{0,1:T(8,128)(2,1)}, u32[]{:S(2)}) copy-start(bf16[384,64]{0,1:T(8,128)(2,1)} %param.3) | copy-start | bytes 147460
  1.8 24.3 %all-to-all-start = ((bf16[16,96,128]{2,1,0:T(8,128)(2,1)}), bf16[16,96,128]{2,1,0:T(8,128)(2,1)S(1)}, u32[]{:S(2)}, u32[]{:S(2)}) async-start(bf16[16,96,128]{2,1,0:T(8,128)(2,1)} %bitcast.1), calls=%async_computation | async-start | bytes 786432 | tf_op jit(solution)/shard_map/all_to_all | solution.py:185
  13.7 2.2 %copy-start = (bf16[512,4096]{1,0:T(8,128)(2,1)S(1)}, bf16[512,4096]{1,0:T(8,128)(2,1)}, u32[]{:S(2)}) copy-start(bf16[512,4096]{1,0:T(8,128)(2,1)} %m_ref.1) | copy-start | bytes 12582916
  15.8 0.7 copy-start.2
  20.2 22.0 %collective-permute-start.3 = (bf16[512,4096]{1,0:T(8,128)(2,1)}, bf16[512,4096]{1,0:T(8,128)(2,1)}, u32[]{:S(2)}, u32[]{:S(2)}) collective-permute-start(bf16[512,4096]{1,0:T(8,128)(2,1)} %shard_map.38.own_ref.m_ref), channel_id=1, source_target_pairs={{0,8},{8,0},{1,9},{9,1},{2,10},{10,2},{3,11},{11,3},{4,12},{12,4},... | collective-permute-start | bytes 12582920 | tf_op jit(solution)/shard_map/ppermute | solution.py:187
  26.1 18.3 %collective-permute-start.2 = (bf16[16,96,128]{2,1,0:T(8,128)(2,1)S(1)}, bf16[16,96,128]{2,1,0:T(8,128)(2,1)S(1)}, u32[]{:S(2)}, u32[]{:S(2)}) collective-permute-start(bf16[16,96,128]{2,1,0:T(8,128)(2,1)S(1)} %all-to-all-done.block_ref), channel_id=1, source_target_pairs={{0,32},{16,48},{32,0},{48,16},{1,33},{17,49},{33,1},{49,17},{2,34}... | collective-permute-start | bytes 1179656 | tf_op jit(solution)/shard_map/ppermute | solution.py:189
  30.7 18.2 %collective-permute-start.1 = (bf16[16,96,128]{2,1,0:T(8,128)(2,1)S(1)}, bf16[16,96,128]{2,1,0:T(8,128)(2,1)S(1)}, u32[]{:S(2)}, u32[]{:S(2)}) collective-permute-start(bf16[16,96,128]{2,1,0:T(8,128)(2,1)S(1)} %all-to-all-done.block_ref), channel_id=1, source_target_pairs={{0,16},{16,32},{32,48},{48,0},{1,17},{17,33},{33,49},{49,1},{2,18}... | collective-permute-start | bytes 1179656 | tf_op jit(solution)/shard_map/ppermute | solution.py:189
  33.0 16.8 %collective-permute-start = (bf16[16,96,128]{2,1,0:T(8,128)(2,1)S(1)}, bf16[16,96,128]{2,1,0:T(8,128)(2,1)S(1)}, u32[]{:S(2)}, u32[]{:S(2)}) collective-permute-start(bf16[16,96,128]{2,1,0:T(8,128)(2,1)S(1)} %all-to-all-done.block_ref), channel_id=1, source_target_pairs={{0,48},{16,0},{32,16},{48,32},{1,49},{17,1},{33,17},{49,33},{2,50}... | collective-permute-start | bytes 1179656 | tf_op jit(solution)/shard_map/ppermute | solution.py:189
